TPU v7x, 32 devices: a whole 2x2x4 slice. The times are simulated.
32 devices in a mesh: ctx: 8 (over y, x, core), tp: 4 (over z).
Axes of the slice: x: 2, y: 2, z: 4, core: 2. Of those that a mesh axis runs over, the one named last changes fastest.
Arguments:
- streams: bfloat16 [3, 2048, 2048], P(None, 'ctx', 'tp'), may hold values from -6 to 6
- short_filter: float32 [3, 7, 2048], P(None, None, 'tp'), may hold values from -2 to 2
- decay_rates: float32 [2048, 16], P('tp'), may hold values from 2.4414063e-05 to 0.05, as said below
- residues: float32 [2048, 16], P('tp'), may hold values from -0.06 to 0.06
- skip_gain: float32 [2048], P('tp'), may hold values from 0.5 to 1.5
- hyena_weight: bfloat16 [2048, 4096], P('tp'), may hold values from -0.1875 to 0.1875
- value_weight: bfloat16 [4096, 2048], P('tp'), may hold values from -0.125 to 0.125
- queries: bfloat16 [2048, 2048], P('ctx', 'tp'), may hold values from -16.5 to 16.5
- key_vectors: bfloat16 [2048, 2048], P('ctx', 'tp'), may hold values from -16.5 to 16.5
Outputs:
- hyena_out: bfloat16 [2048, 4096], P('ctx', 'tp')
- context: bfloat16 [2048, 2048], P('ctx', 'tp')
Inputs may be any that keep to these rules, and one draw needn't show every extreme that they name: `decay_rates`: decay rates lie between 1 / 40960 and 0.05.
All inputs are finite; a program needn't handle non-finite values.
Results may differ from a plain program's by a relative error of at most 0.0066.
Values may be sent and summed in bfloat16 or wider, within the bound.
A program may use at most 128 MiB of HBM per device.

v0:
```python
import math

import jax
import jax.numpy as jnp
from jax import lax
from jax.sharding import PartitionSpec as P

HD = 128


def from_behind(value, axis, steps):
    count = lax.axis_size(axis)
    initial, last = (max(0, -steps), min(count, count - steps))
    return lax.ppermute(value, axis, [(source, source + steps) for source in range(initial, last)])


def carried_in(value, axis, join, neutral):
    count, mine = (lax.axis_size(axis), lax.axis_index(axis))
    pieces = jax.tree.map(lambda part: lax.all_gather(part, axis), value)
    so_far = jax.tree.map(
        lambda part, zero: jnp.full_like(part, 0) + jnp.asarray(zero, part.dtype), value, neutral
    )

    def lap(position, so_far):
        longer = join(so_far, jax.tree.map(lambda part: part[position], pieces))
        return jax.tree.map(lambda new, old: jnp.where(position < mine, new, old), longer, so_far)

    return lax.fori_loop(0, count - 1, lap, so_far)


def chain_link(earlier, later):
    return (earlier[0] * later[0], later[0] * earlier[1] + later[1])


def hyena_mixer(streams, short_filter, decay_rates, residues, skip_gain, hyena_weight):
    tok_rows = streams.shape[1]
    previous = from_behind(streams[:, tok_rows - 6 :, :], "ctx", 1)
    extended = jnp.concatenate([previous, streams], axis=1).astype(jnp.float32)
    filtered = jnp.zeros((3, tok_rows, streams.shape[2]), jnp.float32)
    for offset in range(7):
        filtered = (
            filtered
            + short_filter[:, offset, None, :] * extended[:, 6 - offset : 6 - offset + tok_rows, :]
        )
    gate_part = filtered[0]
    product = filtered[1] * filtered[2]
    pole_state = product[:, :, None] * jnp.ones((1, 1, decay_rates.shape[1]), jnp.float32)
    stride = 1
    while stride < tok_rows:
        earlier_rows = jnp.pad(pole_state[: tok_rows - stride], ((stride, 0), (0, 0), (0, 0)))
        pole_state = pole_state + jnp.exp(-decay_rates * stride)[None] * earlier_rows
        stride = stride * 2
    end_state = pole_state[tok_rows - 1]
    block_decay = jnp.exp(-decay_rates * tok_rows)
    scanned = carried_in(
        (block_decay, end_state),
        "ctx",
        chain_link,
        (jnp.ones_like(block_decay), jnp.zeros_like(end_state)),
    )
    incoming = scanned[1]
    local_steps = (jnp.arange(tok_rows) + 1).astype(jnp.float32)
    pole_state = (
        pole_state + jnp.exp(-decay_rates[None] * local_steps[:, None, None]) * incoming[None]
    )
    longconv = jnp.sum(pole_state * residues[None], axis=2)
    gated = (gate_part * (longconv + skip_gain[None, :] * product)).astype(jnp.bfloat16)
    every_channel = lax.all_gather(gated, "tp", axis=1, tiled=True)
    column_rows = lax.all_to_all(hyena_weight, "tp", split_axis=1, concat_axis=0, tiled=True)
    summed = jnp.dot(every_channel, column_rows, preferred_element_type=jnp.float32)
    return summed.astype(jnp.bfloat16)


def attend_block(running, key_block, value_block, key_start, query_heads, query_index):
    rows_here = key_block.shape[0]
    head_count = query_heads.shape[1]
    scale = 1.0 / math.sqrt(HD)
    key_heads = key_block.reshape(rows_here, head_count, HD)
    value_heads = value_block.reshape(rows_here, head_count, HD)
    scores = (
        jnp.einsum("qhd,khd->hqk", query_heads, key_heads, preferred_element_type=jnp.float32)
        * scale
    )
    key_index = key_start + jnp.arange(rows_here)
    allowed = (key_index[None, :] <= query_index[:, None])[None]
    top_old, total_old, summed_old = running
    top_new = jnp.maximum(top_old, jnp.max(jnp.where(allowed, scores, -1e30), axis=2))
    weights = jnp.where(allowed, jnp.exp(scores - top_new[:, :, None]), 0.0)
    rescale = jnp.exp(top_old - top_new)
    total_new = total_old * rescale + jnp.sum(weights, axis=2)
    added = jnp.einsum(
        "hqk,khd->hqd",
        weights.astype(jnp.bfloat16),
        value_heads,
        preferred_element_type=jnp.float32,
    )
    return (top_new, total_new, summed_old * rescale[:, :, None] + added)


def fold_piece(running, key_piece, value_piece, step_fn):
    piece_rows = key_piece.shape[0]
    block_total = piece_rows // 512
    key_blocks = key_piece.reshape(block_total, 512, key_piece.shape[1])
    value_blocks = value_piece.reshape(block_total, 512, value_piece.shape[1])
    block_starts = 512 * jnp.arange(block_total)

    def scan_step(state_now, inputs):
        return (step_fn(state_now, inputs[0], inputs[1], inputs[2]), None)

    result, unused = lax.scan(scan_step, running, (key_blocks, value_blocks, block_starts))
    return result


def start_state(head_count, rows):
    return (
        jnp.full((head_count, rows), -1e30, jnp.float32),
        jnp.zeros((head_count, rows), jnp.float32),
        jnp.zeros((head_count, rows, HD), jnp.float32),
    )


def finish_state(state):
    top_final, total_final, summed_final = state
    rows = summed_final.shape[1]
    normalized = summed_final / total_final[:, :, None]
    return (
        normalized.transpose(1, 0, 2).reshape(rows, summed_final.shape[0] * HD).astype(jnp.bfloat16)
    )


def causal_attention(queries, key_vectors, values):
    tok_rows = queries.shape[0]
    head_count = queries.shape[1] // HD
    position = lax.axis_index("ctx")
    query_heads = queries.reshape(tok_rows, head_count, HD)
    query_index = position * tok_rows + jnp.arange(tok_rows)

    def step_fn(state_now, key_block, value_block, key_start):
        return attend_block(state_now, key_block, value_block, key_start, query_heads, query_index)

    initial = start_state(head_count, tok_rows)
    final_state = fold_piece(
        initial,
        lax.all_gather(key_vectors, "ctx", axis=0, tiled=True),
        lax.all_gather(values, "ctx", axis=0, tiled=True),
        step_fn,
    )
    return finish_state(final_state)


def shards(
    streams,
    short_filter,
    decay_rates,
    residues,
    skip_gain,
    hyena_weight,
    value_weight,
    queries,
    key_vectors,
):
    hyena_out = hyena_mixer(streams, short_filter, decay_rates, residues, skip_gain, hyena_weight)
    value_terms = jnp.dot(hyena_out, value_weight, preferred_element_type=jnp.float32)
    values = lax.psum_scatter(value_terms, "tp", scatter_dimension=1, tiled=True).astype(
        jnp.bfloat16
    )
    context = causal_attention(queries, key_vectors, values)
    return (hyena_out, context)


def solution(mesh):
    return jax.shard_map(
        shards,
        mesh=mesh,
        in_specs=(
            P(None, "ctx", "tp"),
            P(None, None, "tp"),
            P("tp", None),
            P("tp", None),
            P("tp"),
            P("tp", None),
            P("tp", None),
            P("ctx", "tp"),
            P("ctx", "tp"),
        ),
        out_specs=(P("ctx", "tp"), P("ctx", "tp")),
        check_vma=False,
    )
```

profile of v0, /device:TPU:15, one launch (start us, length us, event | category | flops | bytes accessed | tf_op | source)
XLA Modules:
  0.0 312.7 jit_solution(2053255607246101564)
XLA Ops:
  10.2 6.5 %copy.36 = bf16[512,4096]{0,1:T(8,128)(2,1)} copy(bf16[512,4096]{1,0:T(8,128)(2,1)} %param.18) | data formatting | bytes 8388608 | tf_op args[5]
  16.7 5.0 %all-to-all-start = ((bf16[512,4,1024]{0,2,1:T(8,128)(2,1)}), bf16[512,4,1024]{0,2,1:T(8,128)(2,1)}, u32[]{:S(2)}, u32[]{:S(2)}) async-start(bf16[512,4,1024]{0,2,1:T(8,128)(2,1)} %bitcast.99), calls=%async_computation | async-start | bytes 8388608 | tf_op jit(solution)/shard_map/all_to_all | solution.py:69
  21.9 10.0 %all-gather = f32[4096,16]{0,1:T(8,128)S(1)} all-gather(f32[512,16]{0,1:T(8,128)S(1)} %get-tuple-element.290), channel_id=2, replica_groups=mesh['ctx'=8,'tp'=4] {'ctx'}, dimensions={0}, use_global_device_ids=true | all-gather | bytes 294912 | tf_op jit(solution)/shard_map/all_gather | solution.py:19
  35.9 4.7 %multiply_add_fusion.7 = f32[256,512,16]{1,2,0:T(8,128)} fusion(f32[255,512,16]{1,2,0:T(8,128)S(1)} %mul.299, f32[512,16]{0,1:T(8,128)S(1)} %get-tuple-element.282, f32[256,512]{1,0:T(8,128)S(1)} %fusion.37), kind=kLoop, calls=%fused_computation.38 | loop fusion | flops 4194304 | bytes 17301504 | tf_op jit(solution)/shard_map/add | solution.py:51
  40.6 4.4 %slice.125 = f32[254,512,16]{1,2,0:T(8,128)S(1)} slice(f32[256,512,16]{1,2,0:T(8,128)} %multiply_add_fusion.7), slice={[0:254], [0:512], [0:16]} | slice | bytes 16646144 | tf_op jit(solution)/shard_map/slice | solution.py:50
  45.1 4.7 %multiply_add_fusion.6 = f32[256,512,16]{1,2,0:T(8,128)} fusion(f32[254,512,16]{1,2,0:T(8,128)S(1)} %slice.125, f32[512,16]{0,1:T(8,128)S(1)} %get-tuple-element.283, f32[255,512,16]{1,2,0:T(8,128)S(1)} %mul.299, f32[512,16]{0,1:T(8,128)S(1)} %get-tuple-element.282, f32[256,512]{1,0:T(8,128)S(1)} %fusion.37), kind=kLoop, calls=%fused_computation.37 | loop fusion | flops 8388608 | bytes 25657344 | tf_op jit(solution)/shard_map/add | solution.py:51
  49.8 8.4 %slice.126 = f32[252,512,16]{1,2,0:T(8,128)} slice(f32[256,512,16]{1,2,0:T(8,128)} %multiply_add_fusion.6), slice={[0:252], [0:512], [0:16]} | slice | bytes 16515072 | tf_op jit(solution)/shard_map/slice | solution.py:50
  58.2 7.4 %multiply_add_fusion.5 = f32[256,512,16]{1,2,0:T(8,128)} fusion(f32[252,512,16]{1,2,0:T(8,128)} %slice.126, f32[512,16]{0,1:T(8,128)S(1)} %get-tuple-element.284, f32[254,512,16]{1,2,0:T(8,128)S(1)} %slice.125, f32[512,16]{0,1:T(8,128)S(1)} %get-tuple-element.283, f32[255,512,16]{1,2,0:T(8,128)S(1)} %mul.299, f32[512,16]{0,1:T(8,128)S(1)} %get-tuple-element.282, ...), kind=kLoop, calls=%fused_computation.36 | loop fusion | flops 12582912 | bytes 33947648 | tf_op jit(solution)/shard_map/add | solution.py:51
  65.6 8.3 %slice.127 = f32[248,512,16]{1,2,0:T(8,128)} slice(f32[256,512,16]{1,2,0:T(8,128)} %multiply_add_fusion.5), slice={[0:248], [0:512], [0:16]} | slice | bytes 16252928 | tf_op jit(solution)/shard_map/slice | solution.py:50
  73.9 12.1 %multiply_add_fusion.4 = f32[256,512,16]{1,2,0:T(8,128)} fusion(f32[256,512,16]{1,2,0:T(8,128)} %multiply_add_fusion.5, f32[248,512,16]{1,2,0:T(8,128)} %slice.127, f32[512,16]{0,1:T(8,128)S(1)} %get-tuple-element.285), kind=kLoop, calls=%fused_computation.35 | loop fusion | flops 4194304 | bytes 24936448 | tf_op jit(solution)/shard_map/add | solution.py:51
  86.0 8.1 %slice.128 = f32[240,512,16]{1,2,0:T(8,128)} slice(f32[256,512,16]{1,2,0:T(8,128)} %multiply_add_fusion.4), slice={[0:240], [0:512], [0:16]} | slice | bytes 15728640 | tf_op jit(solution)/shard_map/slice | solution.py:50
  94.1 12.0 %multiply_add_fusion.3 = f32[256,512,16]{1,2,0:T(8,128)} fusion(f32[256,512,16]{1,2,0:T(8,128)} %multiply_add_fusion.4, f32[240,512,16]{1,2,0:T(8,128)} %slice.128, f32[512,16]{0,1:T(8,128)S(1)} %get-tuple-element.286), kind=kLoop, calls=%fused_computation.34 | loop fusion | flops 4194304 | bytes 24674304 | tf_op jit(solution)/shard_map/add | solution.py:51
  106.0 7.7 %slice.129 = f32[224,512,16]{1,2,0:T(8,128)} slice(f32[256,512,16]{1,2,0:T(8,128)} %multiply_add_fusion.3), slice={[0:224], [0:512], [0:16]} | slice | bytes 14680064 | tf_op jit(solution)/shard_map/slice | solution.py:50
  113.7 11.7 %multiply_add_fusion.2 = f32[256,512,16]{1,2,0:T(8,128)} fusion(f32[256,512,16]{1,2,0:T(8,128)} %multiply_add_fusion.3, f32[224,512,16]{1,2,0:T(8,128)} %slice.129, f32[512,16]{0,1:T(8,128)S(1)} %get-tuple-element.287), kind=kLoop, calls=%fused_computation.33 | loop fusion | flops 4194304 | bytes 24150016 | tf_op jit(solution)/shard_map/add | solution.py:51
  125.5 2.8 slice-done
  128.2 8.7 %multiply_add_fusion.1 = f32[256,512,16]{1,2,0:T(8,128)} fusion(f32[256,512,16]{1,2,0:T(8,128)} %multiply_add_fusion.2, f32[192,512,16]{1,2,0:T(8,128)S(1)} %slice-done, f32[512,16]{0,1:T(8,128)S(1)} %get-tuple-element.288), kind=kLoop, calls=%fused_computation.32 | loop fusion | flops 4194304 | bytes 23101440 | tf_op jit(solution)/shard_map/add | solution.py:51
  137.0 2.2 slice-done.1
  139.2 8.9 %multiply_add_fusion = f32[256,512,16]{1,2,0:T(8,128)} fusion(f32[256,512,16]{1,2,0:T(8,128)} %multiply_add_fusion.1, f32[128,512,16]{1,2,0:T(8,128)S(1)} %slice-done.1, f32[512,16]{0,1:T(8,128)S(1)} %get-tuple-element.289), kind=kLoop, calls=%fused_computation.31 | loop fusion | flops 4194304 | bytes 21004288 | tf_op jit(solution)/shard_map/add | solution.py:51
  149.0 9.1 %all_gather.20 = f32[8,512,16]{1,2,0:T(8,128)S(1)} all-gather(f32[1,512,16]{1,2,0:T(8,128)S(1)} %slice.132), channel_id=1, replica_groups=mesh['ctx'=8,'tp'=4] {'ctx'}, dimensions={0}, use_global_device_ids=true | all-gather | bytes 294912 | tf_op jit(solution)/shard_map/all_gather | solution.py:19
  158.6 5.2 %multiply_reduce_fusion = f32[256,512]{1,0:T(8,128)S(1)} fusion(f32[256,512,16]{1,2,0:T(8,128)} %multiply_add_fusion, f32[512,16]{0,1:T(8,128)S(1)} %copy-done.5, f32[512,16]{0,1:T(8,128)S(1)} %get-tuple-element.144, f32[256]{0:T(256)S(1)} %add_convert_fusion, f32[512,16]{0,1:T(8,128)S(1)} %get-tuple-element.281), kind=kLoop, calls=%fused_computation.30 | loop fusion | flops 10354688 | bytes 9012224 | tf_op jit(solution)/shard_map/reduce_sum | solution.py:66
  164.8 6.3 %copy.37 = bf16[4,512,1024]{2,1,0:T(8,128)(2,1)} copy(bf16[4,512,1024]{1,2,0:T(8,128)(2,1)} %bitcast.4) | data formatting | bytes 8388608 | tf_op jit(solution)/shard_map/all_to_all | solution.py:69
  171.1 21.8 %all-gather.5.cloned.1.call-done = bf16[256,2048]{1,0:T(8,128)(2,1)} async-done(((bf16[256,512]{1,0:T(8,128)(2,1)}), bf16[256,2048]{1,0:T(8,128)(2,1)}) %all-gather.5.cloned.1.call-update) | async-done | bytes 1048592 | tf_op jit(solution)/shard_map/all_gather | solution.py:68
  193.0 3.8 %convolution_convert_fusion = bf16[256,1024]{1,0:T(8,128)(2,1)S(1)} fusion(bf16[256,2048]{1,0:T(8,128)(2,1)} %all-gather.5.cloned.1.call-done, bf16[2048,1024]{1,0:T(8,128)(2,1)} %bitcast.101), kind=kOutput, calls=%fused_computation.52 | convolution fusion | flops 1074003968 | bytes 5767168 | tf_op jit(solution)/shard_map/dot_general | solution.py:70
  197.6 4.8 %fusion.29 = f32[256,2048]{1,0:T(8,128)} fusion(bf16[256,1024]{1,0:T(8,128)(2,1)S(1)} %convolution_convert_fusion, bf16[1024,2048]{1,0:T(8,128)(2,1)} %param.19), kind=kOutput, calls=%fused_computation.82 | convolution fusion | flops 1073741824 | bytes 6815744 | tf_op jit(solution)/shard_map/dot_general | solution.py:163
  203.0 40.7 %reduce-scatter.2.cloned.1.call-done = f32[256,512]{1,0:T(8,128)} async-done(((f32[256,2048]{1,0:T(8,128)}), f32[256,512]{1,0:T(8,128)}) %reduce-scatter.2.cloned.1.call-update) | async-done | bytes 524304 | tf_op jit(solution)/shard_map/reduce_scatter | solution.py:164
  243.8 1.8 convert_element_type.51
  246.5 28.1 %all-gather.9.cloned.1.call-done = bf16[2048,512]{1,0:T(8,128)(2,1)} async-done(((bf16[256,512]{1,0:T(8,128)(2,1)}), bf16[2048,512]{1,0:T(8,128)(2,1)}) %all-gather.9.cloned.1.call-update) | async-done | bytes 2097168 | tf_op jit(solution)/shard_map/all_gather | solution.py:145
  274.6 28.7 %while.30 = (s32[]{:T(128)}, f32[4,256]{1,0:T(4,128)S(1)}, f32[4,256]{1,0:T(4,128)S(1)}, f32[4,256,128]{2,1,0:T(8,128)}, s32[4]{0:T(128)}, /*index=5*/bf16[4,512...) while((s32[]{:T(128)}, f32[4,256]{1,0:T(4,128)S(1)}, ...), condition=%wide.region_7.8_spmd.clone, body=%wide.region_4.7_spmd.clone.sunk | while | flops 274732800 | bytes 13441169 | solution.py:110
  285.8 2.6 convolution_add_fusion.2
  293.3 2.6 convolution_add_fusion.2
  300.7 2.6 convolution_add_fusion.2
  303.4 2.0 copy_bitcast_fusion.1
  (120 shorter events, 31.9 us)
Async XLA Ops:
  8.7 13.0 %copy-start.4 = (f32[3,7,512]{2,1,0:T(8,128)S(1)}, f32[3,7,512]{2,1,0:T(8,128)}, u32[]{:S(2)}) copy-start(f32[3,7,512]{2,1,0:T(8,128)} %param.14) | copy-start | bytes 129028
  8.8 13.0 %copy-start.6 = (f32[512,16]{0,1:T(8,128)S(1)}, f32[512,16]{0,1:T(8,128)}, u32[]{:S(2)}) copy-start(f32[512,16]{0,1:T(8,128)} %param.15) | copy-start | bytes 98308
  8.8 23.3 %copy-start.2 = (bf16[3,256,512]{2,1,0:T(8,128)(2,1)S(1)}, bf16[3,256,512]{2,1,0:T(8,128)(2,1)}, u32[]{:S(2)}) copy-start(bf16[3,256,512]{2,1,0:T(8,128)(2,1)} %param.13) | copy-start | bytes 2359300
  8.8 23.3 %collective-permute-start = (bf16[3,6,512]{2,1,0:T(8,128)(2,1)S(1)}, bf16[3,6,512]{2,1,0:T(8,128)(2,1)S(1)}, u32[]{:S(2)}, u32[]{:S(2)}) collective-permute-start(bf16[3,6,512]{2,1,0:T(8,128)(2,1)S(1)} %slice.87), channel_id=1, source_target_pairs={{0,4},{4,8},{8,12},{12,16},{16,20},{20,24},{24,28},{1,5},{5,9},{9,... | collective-permute-start | bytes 55304 | tf_op jit(solution)/shard_map/ppermute | solution.py:14
  16.7 148.1 %all-to-all-start = ((bf16[512,4,1024]{0,2,1:T(8,128)(2,1)}), bf16[512,4,1024]{0,2,1:T(8,128)(2,1)}, u32[]{:S(2)}, u32[]{:S(2)}) async-start(bf16[512,4,1024]{0,2,1:T(8,128)(2,1)} %bitcast.99), calls=%async_computation | async-start | bytes 8388608 | tf_op jit(solution)/shard_map/all_to_all | solution.py:69
  21.7 171.3 %all-gather.5.cloned.1.call-start = ((), (), s32[]{:S(2)}) async-start(), calls=%async_computation.2 | async-start | bytes 1310720 | tf_op jit(solution)/shard_map/all_gather | solution.py:68
  33.6 1.2 copy-start
  125.5 2.8 slice-start
  137.0 2.2 slice-start.1
  139.2 19.5 %copy-start.5 = (f32[512,16]{0,1:T(8,128)S(1)}, f32[512,16]{0,1:T(8,128)}, u32[]{:S(2)}) copy-start(f32[512,16]{0,1:T(8,128)} %param.16) | copy-start | bytes 98308
  148.1 15.7 %copy-start.1 = (f32[3,256,512]{2,1,0:T(8,128)S(1)}, f32[3,256,512]{2,1,0:T(8,128)}, u32[]{:S(2)}) copy-start(f32[3,256,512]{2,1,0:T(8,128)} %copy-done) | copy-start | bytes 4718596
  148.1 15.7 %copy-start.7 = (f32[512]{0:T(512)S(1)}, f32[512]{0:T(512)}, u32[]{:S(2)}) copy-start(f32[512]{0:T(512)} %param.17) | copy-start | bytes 6148
  164.8 79.0 %reduce-scatter.2.cloned.1.call-start = ((), (), s32[]{:S(2)}) async-start(), calls=%async_computation.4 | async-start | bytes 2621440 | tf_op jit(solution)/shard_map/reduce_scatter | solution.py:164
  193.0 52.6 %copy-start.3 = (bf16[256,512]{1,0:T(8,128)(2,1)S(1)}, bf16[256,512]{1,0:T(8,128)(2,1)}, u32[]{:S(2)}) copy-start(bf16[256,512]{1,0:T(8,128)(2,1)} %param.20) | copy-start | bytes 786436
  196.8 0.8 copy-start.8
  202.4 44.1 %all-gather.7.cloned.1.call-start = ((), (), s32[]{:S(2)}) async-start(), calls=%async_computation.3 | async-start | bytes 2359296 | tf_op jit(solution)/shard_map/all_gather | solution.py:144
  203.0 71.6 %all-gather.9.cloned.1.call-start = ((), (), s32[]{:S(2)}) async-start(), calls=%async_computation.5 | async-start | bytes 2359296 | tf_op jit(solution)/shard_map/all_gather | solution.py:145
Sparse Core Ops, SparseCore 0:
  164.9 28.0 all-gather.4
  202.5 41.2 reduce-scatter.1
Sparse Core Ops, SparseCore 1:
  204.7 27.0 all-gather.6
  245.6 28.9 all-gather.8
where the time goes:
time: 316 us; the launch traced here: 313 us
  waiting for transfers between devices  91.3 us (29%)
  other arithmetic  87.6 us (28%)
  local copies, waits for them, and re-layouts  71.7 us (23%)
  matrix products  20.3 us (6%)
  blocking collectives  19.1 us (6%)
  between operations  15.8 us (5%)
  starting transfers between devices  6.53 us (2%)
    add x8, other arithmetic, hyena_mixer(): pole_state + jnp.exp(-decay_rates * stride)[None] * earlier_rows  70.3 us
    slice x10, local copies, waits for them, and re-layouts, hyena_mixer(): pole_state[:tok_rows - stride]  42 us
    reduce_scatter x1, waiting for transfers between devices, shards(): lax.psum_scatter(value_terms, 'tp', scatter_dimension=1, tiled=True)  40.7 us
    all_gather x1, waiting for transfers between devices, causal_attention(): lax.all_gather(values, 'ctx', axis=0, tiled=True)  28.1 us
    all_gather x1, waiting for transfers between devices, hyena_mixer(): every_channel = lax.all_gather(gated, 'tp', axis=1, tiled=True)  21.8 us
    all_gather x2, blocking collectives, carried_in(): pieces = jax.tree.map(lambda part: lax.all_gather(part, axis), value)  19.1 us
    dynamic_slice x16, local copies, waits for them, and re-layouts, fold_piece(): lax.scan(scan_step, running, (key_blocks, value_blocks, block_starts))  11.7 us
    dot_general x4, matrix products, attend_block(): jnp.einsum('hqk,khd->hqd', weights.astype(jnp.bfloat16), value_heads, pre...  9.45 us
  transfers between devices with their start and end apart: 6, of which 3 were waited for; matrix products, arithmetic and copies ran while one was open for 43% of the time, Pallas kernels for 0%

commit v1 on v0

v1 whole, which is shorter than its diff:
```python
import functools
import math

import jax
import jax.numpy as jnp
from jax import lax
from jax.experimental import pallas as pl
from jax.experimental.pallas import tpu as pltpu
from jax.sharding import PartitionSpec as P

HD = 128
LANES = 128
SEGS = 8
HALO = 16
KEYS = 512


def from_behind(value, axis, steps):
    count = lax.axis_size(axis)
    initial, last = (max(0, -steps), min(count, count - steps))
    return lax.ppermute(value, axis, [(source, source + steps) for source in range(initial, last)])


def filter_kernel(prev_ref, streams_ref, taps_ref, rates_ref, gate_ref, u_ref, seg_ref, end_ref, ext):
    rows = streams_ref.shape[1]
    steps = rows // SEGS
    modes = rates_ref.shape[0]
    outs = []
    for s in range(3):
        ext[s, :HALO, :] = prev_ref[s].astype(jnp.float32)
        ext[s, HALO:, :] = streams_ref[s].astype(jnp.float32)
    for s in range(3):
        acc = taps_ref[s, 0:1, :] * ext[s, HALO:, :]
        for j in range(1, 7):
            acc = acc + taps_ref[s, j : j + 1, :] * ext[s, HALO - j : HALO - j + rows, :]
        outs.append(acc)
    gate_ref[...] = outs[0]
    u_ref[...] = outs[1] * outs[2]
    rates = rates_ref[...]
    decay = jnp.exp(-rates)
    factor = [jnp.broadcast_to(decay[n : n + 1], (SEGS, LANES)) for n in range(modes)]
    state = [jnp.zeros((SEGS, LANES), jnp.float32) for _ in range(modes)]
    for step in range(steps):
        here = u_ref[pl.ds(step, SEGS, stride=steps), :]
        for n in range(modes):
            state[n] = state[n] * factor[n] + here
    left = (steps * (SEGS - 1 - lax.broadcasted_iota(jnp.int32, (SEGS, LANES), 0))).astype(jnp.float32)
    for n in range(modes):
        seg_ref[n * SEGS : (n + 1) * SEGS, :] = state[n]
        reach = jnp.exp(-jnp.broadcast_to(rates[n : n + 1], (SEGS, LANES)) * left)
        end_ref[n : n + 1, :] = jnp.sum(reach * state[n], axis=0, keepdims=True)


def mix_kernel(gate_ref, u_ref, seg_ref, inc_ref, rates_ref, res_ref, skip_ref, out_ref, first, mixed):
    rows = u_ref.shape[0]
    steps = rows // SEGS
    modes = rates_ref.shape[0]
    rates = rates_ref[...]
    decay = jnp.exp(-rates)
    hop = jnp.exp(-rates * steps)
    carried = inc_ref[...]
    for seg in range(SEGS):
        first[pl.ds(seg, modes, stride=SEGS), :] = carried
        carried = carried * hop + seg_ref[pl.ds(seg, modes, stride=SEGS), :]
    residue = res_ref[...]
    skip = jnp.broadcast_to(skip_ref[...], (SEGS, LANES))
    factor = [jnp.broadcast_to(decay[n : n + 1], (SEGS, LANES)) for n in range(modes)]
    weight = [jnp.broadcast_to(residue[n : n + 1], (SEGS, LANES)) for n in range(modes)]
    state = [first[n * SEGS : (n + 1) * SEGS, :] for n in range(modes)]
    for step in range(steps):
        where = pl.ds(step, SEGS, stride=steps)
        here = u_ref[where, :]
        terms = [skip * here, None]
        for n in range(modes):
            state[n] = state[n] * factor[n] + here
            term = weight[n] * state[n]
            terms[n % 2] = term if terms[n % 2] is None else terms[n % 2] + term
        mixed[where, :] = gate_ref[where, :] * (terms[0] + terms[1])
    out_ref[...] = mixed[...].astype(jnp.bfloat16)


def hyena_gated(streams, short_filter, rates, residues, skip_gain):
    rows, chans = streams.shape[1:]
    modes = rates.shape[0]
    blocks = chans // LANES
    previous = from_behind(streams[:, rows - HALO :, :], "ctx", 1)
    f32 = jnp.float32
    tok = pl.BlockSpec((rows, LANES), lambda i: (0, i))
    pole = pl.BlockSpec((modes, LANES), lambda i: (0, i))
    seg = pl.BlockSpec((modes * SEGS, LANES), lambda i: (0, i))
    gate, u, seg_state, end_state = pl.pallas_call(
        filter_kernel,
        grid=(blocks,),
        in_specs=[
            pl.BlockSpec((3, HALO, LANES), lambda i: (0, 0, i)),
            pl.BlockSpec((3, rows, LANES), lambda i: (0, 0, i)),
            pl.BlockSpec((3, 7, LANES), lambda i: (0, 0, i)),
            pole,
        ],
        out_specs=[tok, tok, seg, pole],
        out_shape=[
            jax.ShapeDtypeStruct((rows, chans), f32),
            jax.ShapeDtypeStruct((rows, chans), f32),
            jax.ShapeDtypeStruct((modes * SEGS, chans), f32),
            jax.ShapeDtypeStruct((modes, chans), f32),
        ],
        scratch_shapes=[pltpu.VMEM((3, rows + HALO, LANES), f32)],
        cost_estimate=pl.CostEstimate(flops=20_000_000, bytes_accessed=2_500_000, transcendentals=0),
        compiler_params=pltpu.CompilerParams(vmem_limit_bytes=24 * 1024 * 1024),
        name="filter_scan",
    )(previous, streams, short_filter, rates)
    count, mine = lax.axis_size("ctx"), lax.axis_index("ctx")
    ends = lax.all_gather(end_state, "ctx")
    gap = mine - 1 - jnp.arange(count)
    reach = jnp.exp(-rates[None] * (rows * jnp.maximum(gap, 0)).astype(f32)[:, None, None])
    incoming = jnp.sum(jnp.where((gap >= 0)[:, None, None], reach * ends, 0.0), axis=0)
    return pl.pallas_call(
        mix_kernel,
        grid=(blocks,),
        in_specs=[tok, tok, seg, pole, pole, pole, pl.BlockSpec((1, LANES), lambda i: (0, i))],
        out_specs=tok,
        out_shape=jax.ShapeDtypeStruct((rows, chans), jnp.bfloat16),
        scratch_shapes=[pltpu.VMEM((modes * SEGS, LANES), f32), pltpu.VMEM((rows, LANES), f32)],
        cost_estimate=pl.CostEstimate(flops=20_000_000, bytes_accessed=2_500_000, transcendentals=0),
        compiler_params=pltpu.CompilerParams(vmem_limit_bytes=24 * 1024 * 1024),
        name="mix_scan",
    )(gate, u, seg_state, incoming, rates, residues, skip_gain[None])


def attend_kernel(pos_ref, q_ref, k_ref, v_ref, out_ref, acc, top, total):
    rows = q_ref.shape[0]
    scale = 1.0 / math.sqrt(HD)
    start = pos_ref[0] * rows
    queries = q_ref[...]
    acc[...] = jnp.zeros_like(acc)
    top[...] = jnp.full_like(top, -1e30)
    total[...] = jnp.zeros_like(total)
    ahead = lax.broadcasted_iota(jnp.int32, (rows, KEYS), 0) - lax.broadcasted_iota(
        jnp.int32, (rows, KEYS), 1
    )

    def block(index, unused):
        at = pl.multiple_of(index * KEYS, KEYS)
        scores = (
            lax.dot_general(
                queries,
                k_ref[pl.ds(at, KEYS), :],
                (((1,), (1,)), ((), ())),
                preferred_element_type=jnp.float32,
            )
            * scale
        )
        scores = jnp.where(ahead >= at - start, scores, -1e30)
        old = top[:, 0:1]
        new = jnp.maximum(old, jnp.max(scores, axis=1, keepdims=True))
        weights = jnp.exp(scores - new)
        rescale = jnp.exp(old - new)
        total[...] = jnp.broadcast_to(
            total[:, 0:1] * rescale + jnp.sum(weights, axis=1, keepdims=True), total.shape
        )
        top[...] = jnp.broadcast_to(new, top.shape)
        acc[...] = acc[...] * rescale + jnp.dot(
            weights.astype(jnp.bfloat16), v_ref[pl.ds(at, KEYS), :], preferred_element_type=jnp.float32
        )
        return unused

    lax.fori_loop(0, (start + rows + KEYS - 1) // KEYS, block, 0)
    out_ref[...] = (acc[...] / total[...]).astype(jnp.bfloat16)


def causal_attention(queries, keys, values):
    rows, width = queries.shape
    length = keys.shape[0]
    own = pl.BlockSpec((rows, HD), lambda h: (0, h))
    every = pl.BlockSpec((length, HD), lambda h: (0, h))
    return pl.pallas_call(
        attend_kernel,
        grid=(width // HD,),
        in_specs=[pl.BlockSpec(memory_space=pltpu.SMEM), own, every, every],
        out_specs=own,
        out_shape=jax.ShapeDtypeStruct((rows, width), jnp.bfloat16),
        scratch_shapes=[pltpu.VMEM((rows, HD), jnp.float32) for _ in range(3)],
        cost_estimate=pl.CostEstimate(
            flops=4 * rows * length * width, bytes_accessed=4 * length * width, transcendentals=0
        ),
        compiler_params=pltpu.CompilerParams(vmem_limit_bytes=32 * 1024 * 1024),
        name="attend",
    )(lax.axis_index("ctx").astype(jnp.int32)[None], queries, keys, values)


def shards(
    streams,
    short_filter,
    decay_rates,
    residues,
    skip_gain,
    hyena_weight,
    value_weight,
    queries,
    key_vectors,
):
    ctx, tp = lax.axis_size("ctx"), lax.axis_size("tp")
    rows = streams.shape[1]
    chans, width = hyena_weight.shape
    gated = hyena_gated(streams, short_filter, decay_rates.T, residues.T, skip_gain)
    every_key = lax.all_gather(key_vectors, "ctx", axis=0, tiled=True)

    piece = width // tp // ctx
    share = lax.dynamic_index_in_dim(
        hyena_weight.reshape(chans, tp, ctx, piece), lax.axis_index("ctx"), 2, keepdims=False
    ).transpose(1, 0, 2)
    share = lax.all_to_all(share, "tp", split_axis=0, concat_axis=0, tiled=True)
    columns = lax.all_gather(share.reshape(tp * chans, piece), "ctx", axis=1, tiled=True)

    every_channel = lax.all_gather(gated, "tp", axis=1, tiled=True)
    hyena_out = jnp.dot(every_channel, columns, preferred_element_type=jnp.float32).astype(
        jnp.bfloat16
    )
    terms = jnp.dot(hyena_out, value_weight, preferred_element_type=jnp.float32).astype(jnp.bfloat16)
    terms = terms.reshape(rows, tp, -1).transpose(1, 0, 2)
    terms = lax.all_to_all(terms, "tp", split_axis=0, concat_axis=0, tiled=True)
    values = jnp.sum(terms.astype(jnp.float32), axis=0).astype(jnp.bfloat16)
    every_value = lax.all_gather(values, "ctx", axis=0, tiled=True)
    context = causal_attention(queries, every_key, every_value)
    return (hyena_out, context)


def solution(mesh):
    return jax.shard_map(
        shards,
        mesh=mesh,
        in_specs=(
            P(None, "ctx", "tp"),
            P(None, None, "tp"),
            P("tp", None),
            P("tp", None),
            P("tp"),
            P("tp", None),
            P("tp", None),
            P("ctx", "tp"),
            P("ctx", "tp"),
        ),
        out_specs=(P("ctx", "tp"), P("ctx", "tp")),
        check_vma=False,
    )
```

time: 316 us -> 195 us (0.62)
  other arithmetic: 87.6 us -> 1.8 us
  local copies, waits for them, and re-layouts: 71.7 us -> 16 us
  blocking collectives: 19.1 us -> 69.1 us
  waiting for transfers between devices: 91.3 us -> 70.9 us
  Pallas kernels: 0 us -> 15.9 us
  matrix products: 20.3 us -> 5.19 us
  starting transfers between devices: 6.53 us -> 1.44 us
    add x21 -> x0, other arithmetic: 74.2 us -> none  [the longest x8 70.3 us: hyena_mixer(): pole_state + jnp.exp(-decay_rates * stride)[None] * earlier_rows]
    all_to_all x0 -> x2, blocking collectives: none -> 57.3 us  [the longest x1 29.5 us: shards(): share = lax.all_to_all(share, 'tp', split_axis=0, concat_axis=0, tiled=True)]
    slice x13 -> x1, local copies, waits for them, and re-layouts: 43.6 us -> 0.81 us  [hyena_gated(): previous = from_behind(streams[:, rows - HALO:, :], 'ctx', 1)]
    reduce_scatter x1 -> x0, waiting for transfers between devices: 40.7 us -> none  [shards(): lax.psum_scatter(value_terms, 'tp', scatter_dimension=1, tiled=True)]
    all_gather x3 -> x4, waiting for transfers between devices: 50 us -> 69 us  [the longest x1 40 us: shards(): lax.all_gather(share.reshape(tp * chans, piece), 'ctx', axis=1, tiled=True)]
    pallas_call x0 -> x3, Pallas kernels: none -> 15.9 us  [the longest x1 11 us: causal_attention(): pl.pallas_call(attend_kernel, grid=(width // HD,), in_specs=[pl.BlockSpec...]
    dot_general x9 -> x1, matrix products: 15.5 us -> 3.9 us  [shards(): jnp.dot(every_channel, columns, preferred_element_type=jnp.float32)]
    dynamic_slice x23 -> x2, local copies, waits for them, and re-layouts: 11.9 us -> 1.35 us  [shards(): lax.dynamic_index_in_dim(hyena_weight.reshape(chans, tp, ctx, piece), lax...]
  transfers between devices with their start and end apart: 6 -> 5, of which waited for: 3 -> 3; matrix products, arithmetic and copies ran while one was open for 43% -> 8% of each run, Pallas kernels for 0% -> 0%
where the time goes in v1:
time: 195 us; the launch traced here: 194 us
  waiting for transfers between devices  70.9 us (36%)
  blocking collectives  69.1 us (35%)
  local copies, waits for them, and re-layouts  16 us (8%)
  Pallas kernels  15.9 us (8%)
  between operations  13.9 us (7%)
  matrix products  5.19 us (3%)
    all_gather x1, waiting for transfers between devices, shards(): lax.all_gather(share.reshape(tp * chans, piece), 'ctx', axis=1, tiled=True)  40 us
    all_to_all x1, blocking collectives, shards(): share = lax.all_to_all(share, 'tp', split_axis=0, concat_axis=0, tiled=True)  29.5 us
    all_gather x1, waiting for transfers between devices, shards(): every_value = lax.all_gather(values, 'ctx', axis=0, tiled=True)  28.9 us
    all_to_all x1, blocking collectives, shards(): terms = lax.all_to_all(terms, 'tp', split_axis=0, concat_axis=0, tiled=True)  27.8 us
    unnamed x21, local copies, waits for them, and re-layouts  13.8 us
    all_gather x1, blocking collectives, hyena_gated(): ends = lax.all_gather(end_state, 'ctx')  11.9 us
    pallas_call x1, Pallas kernels, causal_attention(): pl.pallas_call(attend_kernel, grid=(width // HD,), in_specs=[pl.BlockSpec...  11 us
  transfers between devices with their start and end apart: 5, of which 3 were waited for; matrix products, arithmetic and copies ran while one was open for 8% of the time, Pallas kernels for 0%

profile of v1, /device:TPU:15, one launch (start us, length us, event | category | flops | bytes accessed | tf_op | source)
XLA Modules:
  0.0 194.3 jit_solution(16586288031693466753)
XLA Ops:
  7.2 0.0 all-gather.6.cloned.1.call-start
  7.2 0.8 slice.3
  8.0 1.3 collective-permute-start
  9.3 0.8 bitcast_negate_fusion
  10.1 1.2 collective-permute-done.prev_ref
  11.3 1.1 copy-done.2
  12.4 0.8 copy-done.3
  13.2 0.8 copy-done.5
  14.0 2.1 %filter_scan.1 = (f32[256,512]{1,0:T(8,128)S(1)}, f32[256,512]{1,0:T(8,128)S(1)}, f32[128,512]{1,0:T(8,128)S(1)}, f32[16,512]{1,0:T(8,128)S(1)}) custom-call(bf16[3,16,512]{2,1,0:T(8,128)(2,1)S(1)} %collective-permute-done.prev_ref, bf16[3,256,512]{2,1,0:T(8,128)(2,1)S(1)} %copy-done.2, f32[3,7,512]{2,1,0:T(8,128)S(1)} %copy-done.5, f32[16,512]{1,0:T(8,128)S(1)} %bitcast.22), custom_call_target="tpu_custom_call" | custom-call | flops 20000000 | bytes 2500000 | tf_op jit(solution)/shard_map/filter_scan/pallas_call | solution.py:91
  16.1 11.9 %all-gather = f32[128,512]{1,0:T(8,128)S(1)} all-gather(f32[16,512]{1,0:T(8,128)S(1)} %get-tuple-element.9), channel_id=2, replica_groups=mesh['ctx'=8,'tp'=4] {'ctx'}, dimensions={0}, use_global_device_ids=true | all-gather | bytes 294912 | tf_op jit(solution)/shard_map/all_gather | solution.py:113
  28.0 0.1 select_reduce_fusion.inc_ref
  28.1 0.7 copy-done.6
  28.8 0.7 copy-done.7
  29.5 2.8 %mix_scan.1 = bf16[256,512]{1,0:T(8,128)(2,1)} custom-call(f32[256,512]{1,0:T(8,128)S(1)} %get-tuple-element.6.gate_ref, f32[256,512]{1,0:T(8,128)S(1)} %get-tuple-element.7.u_ref, f32[128,512]{1,0:T(8,128)S(1)} %get-tuple-element.8.seg_ref, f32[16,512]{1,0:T(8,128)S(1)} %select_reduce_fusion.inc_ref, f32[16,512]{1,0:T(8,128)S(1)} %bitcast.23, ...), custom_call_target="tpu_custom_call" | custom-call | flops 20000000 | bytes 2500000 | tf_op jit(solution)/shard_map/mix_scan/pallas_call | solution.py:117
  32.3 0.0 all-gather.8.cloned.1.call-start
  32.4 6.5 %copy.13 = bf16[512,4096]{0,1:T(8,128)(2,1)} copy(bf16[512,4096]{1,0:T(8,128)(2,1)} %param.14) | data formatting | bytes 8388608 | tf_op args[5]
  38.8 1.1 constant_dynamic-slice_fusion
  39.9 0.3 copy.14
  40.2 29.5 %all_to_all.10 = bf16[4,512,128]{2,1,0:T(8,128)(2,1)} all-to-all(bf16[4,512,128]{2,1,0:T(8,128)(2,1)S(1)} %bitcast.29), channel_id=1, replica_groups=mesh['ctx'=8,'tp'=4] {'tp'}, dimensions={0} | all-to-all | bytes 1048576 | tf_op jit(solution)/shard_map/all_to_all | solution.py:212
  69.7 0.0 all-gather.10.cloned.1.call-start
  69.7 0.7 all-gather.10.cloned.1.call-update
  70.4 0.0 all-gather.12.cloned.1.call-start
  70.5 40.0 %all-gather.8.cloned.1.call-done = bf16[2048,1024]{1,0:T(8,128)(2,1)} async-done(((bf16[2048,128]{1,0:T(8,128)(2,1)}), bf16[2048,1024]{1,0:T(8,128)(2,1)}) %all-gather.8.cloned.1.call-update) | async-done | bytes 4194320 | tf_op jit(solution)/shard_map/all_gather | solution.py:213
  110.5 3.9 %convolution_convert_fusion.1 = bf16[256,1024]{1,0:T(8,128)(2,1)S(1)} fusion(bf16[256,2048]{1,0:T(8,128)(2,1)} %all-gather.6.cloned.1.call-done, bf16[2048,1024]{1,0:T(8,128)(2,1)} %all-gather.8.cloned.1.call-done), kind=kOutput, calls=%fused_computation.1 | convolution fusion | flops 1074003968 | bytes 5767168 | tf_op jit(solution)/shard_map/dot_general | solution.py:216
  114.5 1.3 convolution_convert_fusion
  115.8 0.1 copy.18
  115.8 27.8 %all_to_all.11 = bf16[4,256,512]{2,1,0:T(8,128)(2,1)S(1)} all-to-all(bf16[4,256,512]{2,1,0:T(8,128)(2,1)S(1)} %bitcast.27), channel_id=1, replica_groups=mesh['ctx'=8,'tp'=4] {'tp'}, dimensions={0} | all-to-all | bytes 2097152 | tf_op jit(solution)/shard_map/all_to_all | solution.py:221
  143.7 0.9 reduce_sum.22
  144.6 28.9 %all-gather.12.cloned.1.call-done.v_ref = bf16[2048,512]{1,0:T(8,128)(2,1)} async-done(((bf16[256,512]{1,0:T(8,128)(2,1)}), bf16[2048,512]{1,0:T(8,128)(2,1)}) %all-gather.12.cloned.1.call-update) | async-done | bytes 2097168 | tf_op jit(solution)/shard_map/all_gather | solution.py:223
  173.5 1.6 copy-done
  175.1 1.6 copy-done.1
  176.7 11.0 %attend.1 = bf16[256,512]{1,0:T(8,128)(2,1)} custom-call(s32[1]{0:T(128)} %bitcast.8.pos_ref, bf16[256,512]{1,0:T(8,128)(2,1)S(1)} %copy-done.4, bf16[2048,512]{1,0:T(8,128)(2,1)S(1)} %copy-done, bf16[2048,512]{1,0:T(8,128)(2,1)S(1)} %copy-done.1), custom_call_target="tpu_custom_call" | custom-call | flops 1073741824 | bytes 4194304 | tf_op jit(solution)/shard_map/attend/pallas_call | solution.py:176
  (20 shorter events, 0.1 us)
Async XLA Ops:
  7.2 63.3 %all-gather.6.cloned.1.call-start = ((), (), s32[]{:S(2)}) async-start(), calls=%async_computation.2 | async-start | bytes 1310720 | tf_op jit(solution)/shard_map/all_gather | solution.py:215
  8.0 3.3 %collective-permute-start = (bf16[3,16,512]{2,1,0:T(8,128)(2,1)S(1)}, bf16[3,16,512]{2,1,0:T(8,128)(2,1)S(1)}, u32[]{:S(2)}, u32[]{:S(2)}) collective-permute-start(bf16[3,16,512]{2,1,0:T(8,128)(2,1)S(1)} %slice.3), channel_id=1, source_target_pairs={{0,4},{4,8},{8,12},{12,16},{16,20},{20,24},{24,28},{1,5},{5,9},{9,... | collective-permute-start | bytes 147464 | tf_op jit(solution)/shard_map/ppermute | solution.py:21
  11.3 1.1 copy-start.2
  12.4 0.8 copy-start.3
  13.2 0.8 copy-start.5
  28.1 0.8 copy-start.6
  28.8 0.7 copy-start.7
  32.3 78.2 %all-gather.8.cloned.1.call-start = ((), (), s32[]{:S(2)}) async-start(), calls=%async_computation.3 | async-start | bytes 4718592 | tf_op jit(solution)/shard_map/all_gather | solution.py:213
  69.7 74.9 %all-gather.10.cloned.1.call-start = ((), (), s32[]{:S(2)}) async-start(), calls=%async_computation.4 | async-start | bytes 2359296 | tf_op jit(solution)/shard_map/all_gather | solution.py:206
  70.4 103.1 %all-gather.12.cloned.1.call-start = ((), (), s32[]{:S(2)}) async-start(), calls=%async_computation.5 | async-start | bytes 2359296 | tf_op jit(solution)/shard_map/all_gather | solution.py:223
  110.5 3.9 %copy-start.8 = (bf16[1024,2048]{1,0:T(8,128)(2,1)S(1)}, bf16[1024,2048]{1,0:T(8,128)(2,1)}, u32[]{:S(2)}) copy-start(bf16[1024,2048]{1,0:T(8,128)(2,1)} %param.15) | copy-start | bytes 12582916
  114.4 1.4 copy-start.9
  115.7 57.8 %copy-start.4 = (bf16[256,512]{1,0:T(8,128)(2,1)S(1)}, bf16[256,512]{1,0:T(8,128)(2,1)}, u32[]{:S(2)}) copy-start(bf16[256,512]{1,0:T(8,128)(2,1)} %q_ref.1) | copy-start | bytes 786436
  173.5 1.6 copy-start
  175.1 1.6 copy-start.1
Sparse Core Ops, SparseCore 0:
  32.4 37.2 all-gather.5
  71.6 38.8 all-gather.7
  112.4 27.8 all-gather.9
  144.7 28.7 all-gather.11

commit v2 on v1

--- a/solution.py
+++ b/solution.py
@@ -12,7 +12,6 @@
 LANES = 128
 SEGS = 8
 HALO = 16
-KEYS = 512
 
 
 def from_behind(value, axis, steps):
@@ -127,65 +126,160 @@
     )(gate, u, seg_state, incoming, rates, residues, skip_gain[None])
 
 
-def attend_kernel(pos_ref, q_ref, k_ref, v_ref, out_ref, acc, top, total):
-    rows = q_ref.shape[0]
+def attend_kernel(
+    ctx, tp, terms_ref, q_ref, k_ref, out_ref, parts, vals, acc, top, total, sum_sems, val_sems
+):
+    rows, width = q_ref.shape
+    heads = width // HD
     scale = 1.0 / math.sqrt(HD)
-    start = pos_ref[0] * rows
-    queries = q_ref[...]
-    acc[...] = jnp.zeros_like(acc)
-    top[...] = jnp.full_like(top, -1e30)
-    total[...] = jnp.zeros_like(total)
-    ahead = lax.broadcasted_iota(jnp.int32, (rows, KEYS), 0) - lax.broadcasted_iota(
-        jnp.int32, (rows, KEYS), 1
-    )
-
-    def block(index, unused):
-        at = pl.multiple_of(index * KEYS, KEYS)
-        scores = (
-            lax.dot_general(
-                queries,
-                k_ref[pl.ds(at, KEYS), :],
-                (((1,), (1,)), ((), ())),
-                preferred_element_type=jnp.float32,
+    me, lane = lax.axis_index("ctx"), lax.axis_index("tp")
+
+    barrier = pltpu.get_barrier_semaphore()
+    for away in range(1, tp):
+        pl.semaphore_signal(
+            barrier,
+            inc=1,
+            device_id={"tp": lax.rem(lane + away, tp)},
+            device_id_type=pl.DeviceIdType.MESH,
+        )
+    for away in range(1, ctx):
+        pl.semaphore_signal(
+            barrier,
+            inc=1,
+            device_id={"ctx": lax.rem(me + away, ctx)},
+            device_id_type=pl.DeviceIdType.MESH,
+        )
+    pl.semaphore_wait(barrier, tp - 1 + ctx - 1)
+
+    def columns(owner, head):
+        return terms_ref.at[:, pl.ds(pl.multiple_of(owner * width + head * HD, HD), HD)]
+
+    def sum_copy(away, head):
+        owner = lax.rem(lane + away, tp)
+        return pltpu.make_async_remote_copy(
+            src_ref=columns(owner, head),
+            dst_ref=parts.at[away - 1, head],
+            send_sem=sum_sems.at[0, away - 1, head],
+            recv_sem=sum_sems.at[1, away - 1, head],
+            device_id={"tp": owner},
+            device_id_type=pl.DeviceIdType.MESH,
+        )
+
+    def val_copy(ahead, head):
+        return pltpu.make_async_remote_copy(
+            src_ref=vals.at[0, head],
+            dst_ref=vals.at[ahead, head],
+            send_sem=val_sems.at[0, ahead, head],
+            recv_sem=val_sems.at[1, ahead, head],
+            device_id={"ctx": lax.rem(me + ahead, ctx)},
+            device_id_type=pl.DeviceIdType.MESH,
+        )
+
+    for head in range(heads):
+        for away in range(1, tp):
+            sum_copy(away, head).start()
+
+    def attend(head):
+        here = slice(head * HD, (head + 1) * HD)
+
+        def fold(behind, diagonal):
+            at = pl.multiple_of((me - behind) * rows, rows)
+            scores = (
+                lax.dot_general(
+                    q_ref[:, here],
+                    k_ref[pl.ds(at, rows), here],
+                    (((1,), (1,)), ((), ())),
+                    preferred_element_type=jnp.float32,
+                )
+                * scale
             )
-            * scale
-        )
-        scores = jnp.where(ahead >= at - start, scores, -1e30)
-        old = top[:, 0:1]
-        new = jnp.maximum(old, jnp.max(scores, axis=1, keepdims=True))
-        weights = jnp.exp(scores - new)
-        rescale = jnp.exp(old - new)
-        total[...] = jnp.broadcast_to(
-            total[:, 0:1] * rescale + jnp.sum(weights, axis=1, keepdims=True), total.shape
-        )
-        top[...] = jnp.broadcast_to(new, top.shape)
-        acc[...] = acc[...] * rescale + jnp.dot(
-            weights.astype(jnp.bfloat16), v_ref[pl.ds(at, KEYS), :], preferred_element_type=jnp.float32
-        )
-        return unused
-
-    lax.fori_loop(0, (start + rows + KEYS - 1) // KEYS, block, 0)
-    out_ref[...] = (acc[...] / total[...]).astype(jnp.bfloat16)
-
-
-def causal_attention(queries, keys, values):
+            if diagonal:
+                query = lax.broadcasted_iota(jnp.int32, (rows, rows), 0)
+                key = lax.broadcasted_iota(jnp.int32, (rows, rows), 1)
+                scores = jnp.where(key <= query, scores, -1e30)
+                new = jnp.max(scores, axis=1, keepdims=True)
+                weights = jnp.exp(scores - new)
+                total[...] = jnp.broadcast_to(jnp.sum(weights, axis=1, keepdims=True), total.shape)
+                kept = 0.0
+            else:
+                old = top[:, 0:1]
+                new = jnp.maximum(old, jnp.max(scores, axis=1, keepdims=True))
+                weights = jnp.exp(scores - new)
+                rescale = jnp.exp(old - new)
+                total[...] = jnp.broadcast_to(
+                    total[:, 0:1] * rescale + jnp.sum(weights, axis=1, keepdims=True), total.shape
+                )
+                kept = acc[...] * rescale
+            top[...] = jnp.broadcast_to(new, top.shape)
+            acc[...] = kept + jnp.dot(
+                weights.astype(jnp.bfloat16), vals[behind, head], preferred_element_type=jnp.float32
+            )
+
+        fold(0, True)
+
+        def earlier(behind, unused):
+            val_copy(behind, head).wait_recv()
+            fold(behind, False)
+            return unused
+
+        lax.fori_loop(1, me + 1, earlier, 0)
+        out_ref[:, here] = (acc[...] / total[...]).astype(jnp.bfloat16)
+
+    for head in range(heads):
+        value = columns(lane, head)[...].astype(jnp.float32)
+        for away in range(1, tp):
+            sum_copy(away, head).wait_recv()
+            value = value + parts[away - 1, head].astype(jnp.float32)
+        vals[0, head] = value.astype(jnp.bfloat16)
+
+        def hand_on(ahead, unused, head=head):
+            val_copy(ahead, head).start()
+            return unused
+
+        lax.fori_loop(1, ctx - me, hand_on, 0)
+        if head >= 1:
+            attend(head - 1)
+    attend(heads - 1)
+
+    for head in range(heads):
+        for away in range(1, tp):
+            sum_copy(away, head).wait_send()
+
+        def sent(ahead, unused, head=head):
+            val_copy(ahead, head).wait_send()
+            return unused
+
+        lax.fori_loop(1, ctx - me, sent, 0)
+
+
+def sum_and_attend(terms, queries, keys):
+    ctx, tp = lax.axis_size("ctx"), lax.axis_size("tp")
     rows, width = queries.shape
-    length = keys.shape[0]
-    own = pl.BlockSpec((rows, HD), lambda h: (0, h))
-    every = pl.BlockSpec((length, HD), lambda h: (0, h))
+    heads = width // HD
     return pl.pallas_call(
-        attend_kernel,
-        grid=(width // HD,),
-        in_specs=[pl.BlockSpec(memory_space=pltpu.SMEM), own, every, every],
-        out_specs=own,
+        functools.partial(attend_kernel, ctx, tp),
+        in_specs=[pl.BlockSpec(memory_space=pltpu.VMEM)] * 3,
+        out_specs=pl.BlockSpec(memory_space=pltpu.VMEM),
         out_shape=jax.ShapeDtypeStruct((rows, width), jnp.bfloat16),
-        scratch_shapes=[pltpu.VMEM((rows, HD), jnp.float32) for _ in range(3)],
+        scratch_shapes=[
+            pltpu.VMEM((tp - 1, heads, rows, HD), jnp.bfloat16),
+            pltpu.VMEM((ctx, heads, rows, HD), jnp.bfloat16),
+            pltpu.VMEM((rows, HD), jnp.float32),
+            pltpu.VMEM((rows, HD), jnp.float32),
+            pltpu.VMEM((rows, HD), jnp.float32),
+            pltpu.SemaphoreType.DMA((2, tp - 1, heads)),
+            pltpu.SemaphoreType.DMA((2, ctx, heads)),
+        ],
         cost_estimate=pl.CostEstimate(
-            flops=4 * rows * length * width, bytes_accessed=4 * length * width, transcendentals=0
+            flops=4 * rows * keys.shape[0] * width,
+            bytes_accessed=4 * keys.shape[0] * width,
+            transcendentals=0,
         ),
-        compiler_params=pltpu.CompilerParams(vmem_limit_bytes=32 * 1024 * 1024),
-        name="attend",
-    )(lax.axis_index("ctx").astype(jnp.int32)[None], queries, keys, values)
+        compiler_params=pltpu.CompilerParams(
+            vmem_limit_bytes=40 * 1024 * 1024, collective_id=0, has_side_effects=True
+        ),
+        name="sum_attend",
+    )(terms, queries, keys)
 
 
 def shards(
@@ -202,26 +296,26 @@
     ctx, tp = lax.axis_size("ctx"), lax.axis_size("tp")
     rows = streams.shape[1]
     chans, width = hyena_weight.shape
+    every_key = lax.all_gather(key_vectors, "ctx", axis=0, tiled=True)
+    piece = width // tp // ctx
+    mine = lax.axis_index("ctx")
+    share = jnp.stack(
+        [
+            lax.dynamic_slice(hyena_weight, (0, (t * ctx + mine) * piece), (chans, piece))
+            for t in range(tp)
+        ]
+    )
+    share = lax.all_to_all(share, "tp", split_axis=0, concat_axis=0, tiled=True)
+    share, streams = lax.optimization_barrier((share, streams))
+    columns = lax.all_gather(share.reshape(tp * chans, piece), "ctx", axis=1, tiled=True)
     gated = hyena_gated(streams, short_filter, decay_rates.T, residues.T, skip_gain)
-    every_key = lax.all_gather(key_vectors, "ctx", axis=0, tiled=True)
-
-    piece = width // tp // ctx
-    share = lax.dynamic_index_in_dim(
-        hyena_weight.reshape(chans, tp, ctx, piece), lax.axis_index("ctx"), 2, keepdims=False
-    ).transpose(1, 0, 2)
-    share = lax.all_to_all(share, "tp", split_axis=0, concat_axis=0, tiled=True)
-    columns = lax.all_gather(share.reshape(tp * chans, piece), "ctx", axis=1, tiled=True)
-
     every_channel = lax.all_gather(gated, "tp", axis=1, tiled=True)
+    every_channel, every_key = lax.optimization_barrier((every_channel, every_key))
     hyena_out = jnp.dot(every_channel, columns, preferred_element_type=jnp.float32).astype(
         jnp.bfloat16
     )
     terms = jnp.dot(hyena_out, value_weight, preferred_element_type=jnp.float32).astype(jnp.bfloat16)
-    terms = terms.reshape(rows, tp, -1).transpose(1, 0, 2)
-    terms = lax.all_to_all(terms, "tp", split_axis=0, concat_axis=0, tiled=True)
-    values = jnp.sum(terms.astype(jnp.float32), axis=0).astype(jnp.bfloat16)
-    every_value = lax.all_gather(values, "ctx", axis=0, tiled=True)
-    context = causal_attention(queries, every_key, every_value)
+    context = sum_and_attend(terms, queries, every_key)
     return (hyena_out, context)
 
 

time: 195 us -> 203 us (1.041)
  blocking collectives: 69.1 us -> 11.9 us
  waiting for transfers between devices: 70.9 us -> 111 us
  Pallas kernels: 15.9 us -> 47 us
  local copies, waits for them, and re-layouts: 16 us -> 5.88 us
  starting transfers between devices: 1.44 us -> 6.12 us
    all_to_all x2 -> x0, blocking collectives: 57.3 us -> none  [the longest x1 29.5 us: shards(): share = lax.all_to_all(share, 'tp', split_axis=0, concat_axis=0, tiled=True)]
    pallas_call x1, Pallas kernels: 11 us -> 42.2 us  [sum_and_attend(): pl.pallas_call(functools.partial(attend_kernel, ctx, tp), in_specs=[pl.Bl...]
    all_gather x1, waiting for transfers between devices: 0.02 us -> 29.1 us  [shards(): every_key = lax.all_gather(key_vectors, 'ctx', axis=0, tiled=True)]
    all_gather x1 -> x0, waiting for transfers between devices: 28.9 us -> none  [shards(): every_value = lax.all_gather(values, 'ctx', axis=0, tiled=True)]
    all_gather x1, waiting for transfers between devices: 0.02 us -> 27.6 us  [shards(): every_channel = lax.all_gather(gated, 'tp', axis=1, tiled=True)]
    unnamed x21, local copies, waits for them, and re-layouts: 13.8 us -> 3.91 us
    all_to_all x0 -> x1, waiting for transfers between devices: none -> 9.83 us  [shards(): share = lax.all_to_all(share, 'tp', split_axis=0, concat_axis=0, tiled=True)]
    all_to_all x0 -> x1, starting transfers between devices: none -> 4.76 us  [shards(): share = lax.all_to_all(share, 'tp', split_axis=0, concat_axis=0, tiled=True)]
  transfers between devices with their start and end apart: 5 -> 5, of which waited for: 3 -> 5; matrix products, arithmetic and copies ran while one was open for 8% -> 0% of each run, Pallas kernels for 0% -> 0%
where the time goes in v2:
time: 203 us
  waiting for transfers between devices  111 us (55%)
  Pallas kernels  47 us (23%)
  between operations  13.9 us (7%)
  blocking collectives  11.9 us (6%)
  starting transfers between devices  6.12 us (3%)
  local copies, waits for them, and re-layouts  5.88 us (3%)
  matrix products  5.17 us (3%)
    pallas_call x1, Pallas kernels, sum_and_attend(): pl.pallas_call(functools.partial(attend_kernel, ctx, tp), in_specs=[pl.Bl...  42.2 us
    all_gather x1, waiting for transfers between devices, shards(): lax.all_gather(share.reshape(tp * chans, piece), 'ctx', axis=1, tiled=True)  39.9 us
    all_gather x1, waiting for transfers between devices, shards(): every_key = lax.all_gather(key_vectors, 'ctx', axis=0, tiled=True)  29.1 us
    all_gather x1, waiting for transfers between devices, shards(): every_channel = lax.all_gather(gated, 'tp', axis=1, tiled=True)  27.6 us
    all_gather x1, blocking collectives, hyena_gated(): ends = lax.all_gather(end_state, 'ctx')  11.9 us
    all_to_all x1, waiting for transfers between devices, shards(): share = lax.all_to_all(share, 'tp', split_axis=0, concat_axis=0, tiled=True)  9.83 us
    all_to_all x1, starting transfers between devices, shards(): share = lax.all_to_all(share, 'tp', split_axis=0, concat_axis=0, tiled=True)  4.76 us
  transfers between devices with their start and end apart: 5, of which 5 were waited for; matrix products, arithmetic and copies ran while one was open for 0% of the time, Pallas kernels for 0%

profile of v2, /device:TPU:15, one launch (start us, length us, event | category | flops | bytes accessed | tf_op | source)
XLA Modules:
  0.0 202.7 jit_solution(16920376172092526853)
XLA Ops:
  7.2 0.0 copy-start.3
  7.2 0.0 copy-start.4
  7.2 1.2 dynamic-slice_bitcast_fusion.3
  8.3 0.9 pad_maximum_fusion
  9.2 4.8 %all-to-all-start = ((bf16[4,512,128]{2,1,0:T(8,128)(2,1)}), bf16[4,512,128]{2,1,0:T(8,128)(2,1)S(1)}, u32[]{:S(2)}, u32[]{:S(2)}) async-start(bf16[4,512,128]{2,1,0:T(8,128)(2,1)} %pad_maximum_fusion), calls=%async_computation | async-start | bytes 1048576 | tf_op jit(solution)/shard_map/all_to_all | solution.py:308
  14.0 0.8 bitcast_negate_fusion
  14.7 9.8 %all-to-all-done = bf16[4,512,128]{2,1,0:T(8,128)(2,1)S(1)} async-done(((bf16[4,512,128]{2,1,0:T(8,128)(2,1)}), bf16[4,512,128]{2,1,0:T(8,128)(2,1)S(1)}, u32[]{:S(2)}, u32[]{:S(2)}) %all-to-all-start) | async-done | bytes 524320 | tf_op jit(solution)/shard_map/all_to_all | solution.py:308
  24.6 0.8 slice.3
  25.4 1.3 collective-permute-start
  26.7 3.2 %collective-permute-done.prev_ref = bf16[3,16,512]{2,1,0:T(8,128)(2,1)S(1)} collective-permute-done((bf16[3,16,512]{2,1,0:T(8,128)(2,1)S(1)}, bf16[3,16,512]{2,1,0:T(8,128)(2,1)S(1)}, u32[]{:S(2)}, u32[]{:S(2)}) %collective-permute-start) | collective-permute-done | bytes 49184 | tf_op jit(solution)/shard_map/ppermute | solution.py:20
  29.9 1.1 copy-done
  31.1 0.8 copy-done.1
  31.8 0.8 copy-done.2
  32.6 2.1 %filter_scan.1 = (f32[256,512]{1,0:T(8,128)S(1)}, f32[256,512]{1,0:T(8,128)S(1)}, f32[128,512]{1,0:T(8,128)S(1)}, f32[16,512]{1,0:T(8,128)S(1)}) custom-call(bf16[3,16,512]{2,1,0:T(8,128)(2,1)S(1)} %collective-permute-done.prev_ref, bf16[3,256,512]{2,1,0:T(8,128)(2,1)S(1)} %copy-done, f32[3,7,512]{2,1,0:T(8,128)S(1)} %copy-done.2, f32[16,512]{1,0:T(8,128)S(1)} %bitcast.18), custom_call_target="tpu_custom_call" | custom-call | flops 20000000 | bytes 2500000 | tf_op jit(solution)/shard_map/filter_scan/pallas_call | solution.py:90
  34.7 11.9 %all-gather = f32[128,512]{1,0:T(8,128)S(1)} all-gather(f32[16,512]{1,0:T(8,128)S(1)} %get-tuple-element.14), channel_id=2, replica_groups=mesh['ctx'=8,'tp'=4] {'ctx'}, dimensions={0}, use_global_device_ids=true | all-gather | bytes 294912 | tf_op jit(solution)/shard_map/all_gather | solution.py:112
  46.6 0.1 select_reduce_fusion.inc_ref
  46.7 2.8 %mix_scan.1 = bf16[256,512]{1,0:T(8,128)(2,1)} custom-call(f32[256,512]{1,0:T(8,128)S(1)} %get-tuple-element.11.gate_ref, f32[256,512]{1,0:T(8,128)S(1)} %get-tuple-element.12.u_ref, f32[128,512]{1,0:T(8,128)S(1)} %get-tuple-element.13.seg_ref, f32[16,512]{1,0:T(8,128)S(1)} %select_reduce_fusion.inc_ref, f32[16,512]{1,0:T(8,128)S(1)} %bitcast.19, ...), custom_call_target="tpu_custom_call" | custom-call | flops 20000000 | bytes 2500000 | tf_op jit(solution)/shard_map/mix_scan/pallas_call | solution.py:116
  49.5 0.0 all-gather.5.cloned.1.call-update
  49.5 0.0 all-gather.7.cloned.1.call-start
  49.6 0.7 all-gather.7.cloned.1.call-update
  50.3 0.0 all-gather.9.cloned.1.call-start
  50.3 0.7 all-gather.9.cloned.1.call-update
  51.0 27.6 %all-gather.5.cloned.1.call-done = bf16[256,2048]{1,0:T(8,128)(2,1)} async-done(((bf16[256,512]{1,0:T(8,128)(2,1)}), bf16[256,2048]{1,0:T(8,128)(2,1)}) %all-gather.5.cloned.1.call-update) | async-done | bytes 1048592 | tf_op jit(solution)/shard_map/all_gather | solution.py:312
  78.6 29.1 %all-gather.7.cloned.1.call-done.k_ref = bf16[2048,512]{1,0:T(8,128)(2,1)} async-done(((bf16[256,512]{1,0:T(8,128)(2,1)}), bf16[2048,512]{1,0:T(8,128)(2,1)}) %all-gather.7.cloned.1.call-update) | async-done | bytes 2097168 | tf_op jit(solution)/shard_map/all_gather | solution.py:299
  107.7 39.9 %all-gather.9.cloned.1.call-done = bf16[2048,1024]{1,0:T(8,128)(2,1)} async-done(((bf16[2048,128]{1,0:T(8,128)(2,1)}), bf16[2048,1024]{1,0:T(8,128)(2,1)}) %all-gather.9.cloned.1.call-update) | async-done | bytes 4194320 | tf_op jit(solution)/shard_map/all_gather | solution.py:310
  147.6 3.9 %convolution_convert_fusion.1 = bf16[256,1024]{1,0:T(8,128)(2,1)S(1)} fusion(bf16[256,2048]{1,0:T(8,128)(2,1)} %all-gather.5.cloned.1.call-done, bf16[2048,1024]{1,0:T(8,128)(2,1)} %all-gather.9.cloned.1.call-done), kind=kOutput, calls=%fused_computation.1 | convolution fusion | flops 1074003968 | bytes 5767168 | tf_op jit(solution)/shard_map/dot_general | solution.py:314
  151.5 0.0 copy-start.9
  151.5 0.0 copy-start.6
  151.5 1.3 convolution_convert_fusion.terms_ref
  152.8 0.5 copy-done.5
  153.3 42.2 %sum_attend.1 = bf16[256,512]{1,0:T(8,128)(2,1)S(1)} custom-call(bf16[256,2048]{1,0:T(8,128)(2,1)S(1)} %convolution_convert_fusion.terms_ref, bf16[256,512]{1,0:T(8,128)(2,1)S(1)} %copy-done.6, bf16[2048,512]{1,0:T(8,128)(2,1)S(1)} %copy-done.5), custom_call_target="tpu_custom_call" | custom-call | flops 1073741824 | bytes 4194304 | tf_op jit(solution)/shard_map/sum_attend/pallas_call | solution.py:259
  195.5 0.7 copy.12
  (15 shorter events, 0.0 us)
Async XLA Ops:
  7.2 39.5 %copy-start.3 = (f32[512,16]{0,1:T(8,128)S(1)}, f32[512,16]{0,1:T(8,128)}, u32[]{:S(2)}) copy-start(f32[512,16]{0,1:T(8,128)} %param.12) | copy-start | bytes 98308
  7.2 39.5 %copy-start.4 = (f32[512]{0:T(512)S(1)}, f32[512]{0:T(512)}, u32[]{:S(2)}) copy-start(f32[512]{0:T(512)} %param.13) | copy-start | bytes 6148
  9.2 15.4 %all-to-all-start = ((bf16[4,512,128]{2,1,0:T(8,128)(2,1)}), bf16[4,512,128]{2,1,0:T(8,128)(2,1)S(1)}, u32[]{:S(2)}, u32[]{:S(2)}) async-start(bf16[4,512,128]{2,1,0:T(8,128)(2,1)} %pad_maximum_fusion), calls=%async_computation | async-start | bytes 1048576 | tf_op jit(solution)/shard_map/all_to_all | solution.py:308
  14.0 64.6 %all-gather.5.cloned.1.call-start = ((), (), s32[]{:S(2)}) async-start(), calls=%async_computation.1 | async-start | bytes 1310720 | tf_op jit(solution)/shard_map/all_gather | solution.py:312
  24.6 25.7 %copy-start.7 = (bf16[4,512,128]{2,1,0:T(8,128)(2,1)}, bf16[4,512,128]{2,1,0:T(8,128)(2,1)S(1)}, u32[]{:S(2)}) copy-start(bf16[4,512,128]{2,1,0:T(8,128)(2,1)S(1)} %all-to-all-done) | copy-start | bytes 1572868
  25.4 4.5 %collective-permute-start = (bf16[3,16,512]{2,1,0:T(8,128)(2,1)S(1)}, bf16[3,16,512]{2,1,0:T(8,128)(2,1)S(1)}, u32[]{:S(2)}, u32[]{:S(2)}) collective-permute-start(bf16[3,16,512]{2,1,0:T(8,128)(2,1)S(1)} %slice.3), channel_id=1, source_target_pairs={{0,4},{4,8},{8,12},{12,16},{16,20},{20,24},{24,28},{1,5},{5,9},{9,... | collective-permute-start | bytes 147464 | tf_op jit(solution)/shard_map/ppermute | solution.py:20
  29.9 1.1 copy-start
  31.1 0.8 copy-start.1
  31.8 0.8 copy-start.2
  49.5 58.1 %all-gather.7.cloned.1.call-start = ((), (), s32[]{:S(2)}) async-start(), calls=%async_computation.2 | async-start | bytes 2359296 | tf_op jit(solution)/shard_map/all_gather | solution.py:299
  50.3 97.3 %all-gather.9.cloned.1.call-start = ((), (), s32[]{:S(2)}) async-start(), calls=%async_computation.3 | async-start | bytes 4718592 | tf_op jit(solution)/shard_map/all_gather | solution.py:310
  147.6 3.9 %copy-start.8 = (bf16[1024,2048]{1,0:T(8,128)(2,1)S(1)}, bf16[1024,2048]{1,0:T(8,128)(2,1)}, u32[]{:S(2)}) copy-start(bf16[1024,2048]{1,0:T(8,128)(2,1)} %param.15) | copy-start | bytes 12582916
  151.5 44.0 %copy-start.9 = (bf16[256,1024]{1,0:T(8,128)(2,1)}, bf16[256,1024]{1,0:T(8,128)(2,1)S(1)}, u32[]{:S(2)}) copy-start(bf16[256,1024]{1,0:T(8,128)(2,1)S(1)} %convolution_convert_fusion.1) | copy-start | bytes 1572868
  151.5 1.8 copy-start.5
  151.5 1.8 copy-start.6
Sparse Core Ops, SparseCore 0:
  49.6 28.9 all-gather.4
  80.5 27.1 all-gather.6
  110.1 37.4 all-gather.8

commit v3 on v2

--- a/solution.py
+++ b/solution.py
@@ -127,7 +127,29 @@
 
 
 def attend_kernel(
-    ctx, tp, terms_ref, q_ref, k_ref, out_ref, parts, vals, acc, top, total, sum_sems, val_sems
+    ctx,
+    tp,
+    gated_ref,
+    share_ref,
+    weight_ref,
+    q_ref,
+    own_ref,
+    hyena_ref,
+    out_ref,
+    gat,
+    full,
+    terms_ref,
+    keys,
+    parts,
+    vals,
+    acc,
+    top,
+    total,
+    gat_sems,
+    full_sems,
+    key_sems,
+    sum_sems,
+    val_sems,
 ):
     rows, width = q_ref.shape
     heads = width // HD
@@ -150,6 +172,70 @@
             device_id_type=pl.DeviceIdType.MESH,
         )
     pl.semaphore_wait(barrier, tp - 1 + ctx - 1)
+
+    def gat_copy(away):
+        return pltpu.make_async_remote_copy(
+            src_ref=gated_ref,
+            dst_ref=gat.at[lane],
+            send_sem=gat_sems.at[0, away],
+            recv_sem=gat_sems.at[1, away],
+            device_id={"tp": lax.rem(lane + away, tp)},
+            device_id_type=pl.DeviceIdType.MESH,
+        )
+
+    def full_copy(away):
+        return pltpu.make_async_remote_copy(
+            src_ref=share_ref,
+            dst_ref=full.at[:, me],
+            send_sem=full_sems.at[0, away],
+            recv_sem=full_sems.at[1, away],
+            device_id={"ctx": lax.rem(me + away, ctx)},
+            device_id_type=pl.DeviceIdType.MESH,
+        )
+
+    def key_copy(ahead):
+        return pltpu.make_async_remote_copy(
+            src_ref=own_ref,
+            dst_ref=keys.at[ahead],
+            send_sem=key_sems.at[0, ahead],
+            recv_sem=key_sems.at[1, ahead],
+            device_id={"ctx": lax.rem(me + ahead, ctx)},
+            device_id_type=pl.DeviceIdType.MESH,
+        )
+
+    for away in range(1, tp):
+        gat_copy(away).start()
+    for away in range(1, ctx):
+        full_copy(away).start()
+
+    def key_on(ahead, unused):
+        key_copy(ahead).start()
+        return unused
+
+    lax.fori_loop(1, ctx - me, key_on, 0)
+    gat[lane] = gated_ref[...]
+    full[:, me] = share_ref[...]
+    keys[0] = own_ref[...]
+    for away in range(1, tp):
+        gat_copy(away).wait_recv()
+    for away in range(1, ctx):
+        full_copy(away).wait_recv()
+    chans, wide = gat.shape[2], full.shape[3]
+    tile = min(wide, 256)
+    for at in range(0, wide, tile):
+        summed = None
+        for p in range(tp):
+            term = jnp.dot(
+                gat[p],
+                full[p, :, :, at : at + tile].reshape(chans, tile),
+                preferred_element_type=jnp.float32,
+            )
+            summed = term if summed is None else summed + term
+        hyena_ref[:, at : at + tile] = summed.astype(jnp.bfloat16)
+    for at in range(0, tp * width, width):
+        terms_ref[:, at : at + width] = jnp.dot(
+            hyena_ref[...], weight_ref[:, at : at + width], preferred_element_type=jnp.float32
+        ).astype(jnp.bfloat16)
 
     def columns(owner, head):
         return terms_ref.at[:, pl.ds(pl.multiple_of(owner * width + head * HD, HD), HD)]
@@ -183,11 +269,10 @@
         here = slice(head * HD, (head + 1) * HD)
 
         def fold(behind, diagonal):
-            at = pl.multiple_of((me - behind) * rows, rows)
             scores = (
                 lax.dot_general(
                     q_ref[:, here],
-                    k_ref[pl.ds(at, rows), here],
+                    keys[behind, :, here],
                     (((1,), (1,)), ((), ())),
                     preferred_element_type=jnp.float32,
                 )
@@ -218,6 +303,8 @@
         fold(0, True)
 
         def earlier(behind, unused):
+            if head == 0:
+                key_copy(behind).wait_recv()
             val_copy(behind, head).wait_recv()
             fold(behind, False)
             return unused
@@ -250,36 +337,56 @@
             return unused
 
         lax.fori_loop(1, ctx - me, sent, 0)
-
-
-def sum_and_attend(terms, queries, keys):
+    for away in range(1, tp):
+        gat_copy(away).wait_send()
+    for away in range(1, ctx):
+        full_copy(away).wait_send()
+
+    def key_sent(ahead, unused):
+        key_copy(ahead).wait_send()
+        return unused
+
+    lax.fori_loop(1, ctx - me, key_sent, 0)
+
+
+def sum_and_attend(gated, share, value_weight, queries, keys):
     ctx, tp = lax.axis_size("ctx"), lax.axis_size("tp")
     rows, width = queries.shape
     heads = width // HD
     return pl.pallas_call(
         functools.partial(attend_kernel, ctx, tp),
-        in_specs=[pl.BlockSpec(memory_space=pltpu.VMEM)] * 3,
-        out_specs=pl.BlockSpec(memory_space=pltpu.VMEM),
-        out_shape=jax.ShapeDtypeStruct((rows, width), jnp.bfloat16),
+        in_specs=[pl.BlockSpec(memory_space=pltpu.VMEM)] * 5,
+        out_specs=[pl.BlockSpec(memory_space=pltpu.VMEM)] * 2,
+        out_shape=[
+            jax.ShapeDtypeStruct((rows, share.shape[2]), jnp.bfloat16),
+            jax.ShapeDtypeStruct((rows, width), jnp.bfloat16),
+        ],
         scratch_shapes=[
+            pltpu.VMEM((tp,) + gated.shape, jnp.bfloat16),
+            pltpu.VMEM((tp, ctx) + share.shape[1:], jnp.bfloat16),
+            pltpu.VMEM((rows, tp * width), jnp.bfloat16),
+            pltpu.VMEM((ctx, rows, width), jnp.bfloat16),
             pltpu.VMEM((tp - 1, heads, rows, HD), jnp.bfloat16),
             pltpu.VMEM((ctx, heads, rows, HD), jnp.bfloat16),
             pltpu.VMEM((rows, HD), jnp.float32),
             pltpu.VMEM((rows, HD), jnp.float32),
             pltpu.VMEM((rows, HD), jnp.float32),
+            pltpu.SemaphoreType.DMA((2, tp)),
+            pltpu.SemaphoreType.DMA((2, ctx)),
+            pltpu.SemaphoreType.DMA((2, ctx)),
             pltpu.SemaphoreType.DMA((2, tp - 1, heads)),
             pltpu.SemaphoreType.DMA((2, ctx, heads)),
         ],
         cost_estimate=pl.CostEstimate(
-            flops=4 * rows * keys.shape[0] * width,
-            bytes_accessed=4 * keys.shape[0] * width,
+            flops=4 * rows * ctx * rows * width,
+            bytes_accessed=4 * ctx * rows * width,
             transcendentals=0,
         ),
         compiler_params=pltpu.CompilerParams(
-            vmem_limit_bytes=40 * 1024 * 1024, collective_id=0, has_side_effects=True
+            vmem_limit_bytes=48 * 1024 * 1024, collective_id=0, has_side_effects=True
         ),
         name="sum_attend",
-    )(terms, queries, keys)
+    )(gated, share, value_weight, queries, keys)
 
 
 def shards(
@@ -296,26 +403,12 @@
     ctx, tp = lax.axis_size("ctx"), lax.axis_size("tp")
     rows = streams.shape[1]
     chans, width = hyena_weight.shape
-    every_key = lax.all_gather(key_vectors, "ctx", axis=0, tiled=True)
-    piece = width // tp // ctx
-    mine = lax.axis_index("ctx")
-    share = jnp.stack(
-        [
-            lax.dynamic_slice(hyena_weight, (0, (t * ctx + mine) * piece), (chans, piece))
-            for t in range(tp)
-        ]
-    )
+    part = chans // ctx
+    share = lax.dynamic_slice(hyena_weight, (lax.axis_index("ctx") * part, 0), (part, width))
+    share = share.reshape(part, tp, width // tp).transpose(1, 0, 2)
     share = lax.all_to_all(share, "tp", split_axis=0, concat_axis=0, tiled=True)
-    share, streams = lax.optimization_barrier((share, streams))
-    columns = lax.all_gather(share.reshape(tp * chans, piece), "ctx", axis=1, tiled=True)
     gated = hyena_gated(streams, short_filter, decay_rates.T, residues.T, skip_gain)
-    every_channel = lax.all_gather(gated, "tp", axis=1, tiled=True)
-    every_channel, every_key = lax.optimization_barrier((every_channel, every_key))
-    hyena_out = jnp.dot(every_channel, columns, preferred_element_type=jnp.float32).astype(
-        jnp.bfloat16
-    )
-    terms = jnp.dot(hyena_out, value_weight, preferred_element_type=jnp.float32).astype(jnp.bfloat16)
-    context = sum_and_attend(terms, queries, every_key)
+    hyena_out, context = sum_and_attend(gated, share, value_weight, queries, key_vectors)
     return (hyena_out, context)
 
 

time: 203 us -> 134 us (0.66)
  waiting for transfers between devices: 111 us -> 1.77 us
  Pallas kernels: 47 us -> 104 us
  between operations: 13.9 us -> 0.77 us
  matrix products: 5.17 us -> 0 us
    all_gather x3 -> x0, waiting for transfers between devices: 96.6 us -> none  [the longest x1 39.9 us: shards(): lax.all_gather(share.reshape(tp * chans, piece), 'ctx', axis=1, tiled=True)]
    pallas_call x1, Pallas kernels: 42.2 us -> 99.9 us  [sum_and_attend(): pl.pallas_call(functools.partial(attend_kernel, ctx, tp), in_specs=[pl.Bl...]
    all_to_all x1, waiting for transfers between devices: 9.83 us -> 0.01 us  [shards(): share = lax.all_to_all(share, 'tp', split_axis=0, concat_axis=0, tiled=True)]
    dot_general x2 -> x0, matrix products: 5.17 us -> none  [the longest x1 3.9 us: shards(): jnp.dot(every_channel, columns, preferred_element_type=jnp.float32)]
    unnamed x21 -> x16, local copies, waits for them, and re-layouts: 3.91 us -> 4.2 us
  transfers between devices with their start and end apart: 5 -> 2, of which waited for: 5 -> 1; matrix products, arithmetic and copies ran while one was open for 0% -> 1% of each run, Pallas kernels for 0% -> 3%
where the time goes in v3:
time: 134 us; the launch traced here: 132 us
  Pallas kernels  104 us (78%)
  blocking collectives  11.9 us (9%)
  local copies, waits for them, and re-layouts  6.97 us (5%)
  starting transfers between devices  6.04 us (5%)
  waiting for transfers between devices  1.77 us (1%)
    pallas_call x1, Pallas kernels, sum_and_attend(): pl.pallas_call(functools.partial(attend_kernel, ctx, tp), in_specs=[pl.Bl...  99.9 us
    all_gather x1, blocking collectives, hyena_gated(): ends = lax.all_gather(end_state, 'ctx')  11.9 us
    all_to_all x1, starting transfers between devices, shards(): share = lax.all_to_all(share, 'tp', split_axis=0, concat_axis=0, tiled=True)  4.76 us
    unnamed x16, local copies, waits for them, and re-layouts  4.2 us
  transfers between devices with their start and end apart: 2, of which 1 were waited for; matrix products, arithmetic and copies ran while one was open for 1% of the time, Pallas kernels for 3%

profile of v3, /device:TPU:15, one launch (start us, length us, event | category | flops | bytes accessed | tf_op | source)
XLA Modules:
  0.0 132.4 jit_solution(8703570025551793535)
XLA Ops:
  0.6 0.0 copy-start.5
  0.6 0.0 copy-start.6
  0.7 0.0 copy-start.2
  0.7 0.0 copy-start.3
  0.7 1.1 constant_dynamic-slice_fusion
  1.8 0.8 copy.14
  2.6 4.8 %all-to-all-start = ((bf16[4,64,1024]{2,1,0:T(8,128)(2,1)}), bf16[4,64,1024]{2,1,0:T(8,128)(2,1)S(1)}, u32[]{:S(2)}, u32[]{:S(2)}) async-start(bf16[4,64,1024]{2,1,0:T(8,128)(2,1)} %bitcast.11), calls=%async_computation | async-start | bytes 1048576 | tf_op jit(solution)/shard_map/all_to_all | solution.py:409
  7.4 0.8 slice.3
  8.2 1.3 collective-permute-start
  9.5 0.8 bitcast_negate_fusion
  10.3 1.8 %collective-permute-done.prev_ref = bf16[3,16,512]{2,1,0:T(8,128)(2,1)S(1)} collective-permute-done((bf16[3,16,512]{2,1,0:T(8,128)(2,1)S(1)}, bf16[3,16,512]{2,1,0:T(8,128)(2,1)S(1)}, u32[]{:S(2)}, u32[]{:S(2)}) %collective-permute-start) | collective-permute-done | bytes 49184 | tf_op jit(solution)/shard_map/ppermute | solution.py:20
  12.1 0.0 copy-start
  12.1 1.1 copy-done
  13.2 0.0 copy-start.1
  13.2 0.8 copy-done.1
  14.0 0.0 copy-start.4
  14.0 0.8 copy-done.4
  14.8 2.1 %filter_scan.1 = (f32[256,512]{1,0:T(8,128)S(1)}, f32[256,512]{1,0:T(8,128)S(1)}, f32[128,512]{1,0:T(8,128)S(1)}, f32[16,512]{1,0:T(8,128)S(1)}) custom-call(bf16[3,16,512]{2,1,0:T(8,128)(2,1)S(1)} %collective-permute-done.prev_ref, bf16[3,256,512]{2,1,0:T(8,128)(2,1)S(1)} %copy-done, f32[3,7,512]{2,1,0:T(8,128)S(1)} %copy-done.4, f32[16,512]{1,0:T(8,128)S(1)} %bitcast.12), custom_call_target="tpu_custom_call" | custom-call | flops 20000000 | bytes 2500000 | tf_op jit(solution)/shard_map/filter_scan/pallas_call | solution.py:90
  16.9 11.9 %all-gather = f32[128,512]{1,0:T(8,128)S(1)} all-gather(f32[16,512]{1,0:T(8,128)S(1)} %get-tuple-element.9), channel_id=2, replica_groups=mesh['ctx'=8,'tp'=4] {'ctx'}, dimensions={0}, use_global_device_ids=true | all-gather | bytes 294912 | tf_op jit(solution)/shard_map/all_gather | solution.py:112
  28.7 0.1 select_reduce_fusion.inc_ref
  28.8 0.0 copy-done.5
  28.8 0.0 copy-done.6
  28.9 2.1 %mix_scan.1.gated_ref = bf16[256,512]{1,0:T(8,128)(2,1)S(1)} custom-call(f32[256,512]{1,0:T(8,128)S(1)} %get-tuple-element.6.gate_ref, f32[256,512]{1,0:T(8,128)S(1)} %get-tuple-element.7.u_ref, f32[128,512]{1,0:T(8,128)S(1)} %get-tuple-element.8.seg_ref, f32[16,512]{1,0:T(8,128)S(1)} %select_reduce_fusion.inc_ref, f32[16,512]{1,0:T(8,128)S(1)} %bitcast.13, ...), custom_call_target="tpu_custom_call" | custom-call | flops 20000000 | bytes 2500000 | tf_op jit(solution)/shard_map/mix_scan/pallas_call | solution.py:116
  30.9 0.0 all-to-all-done.share_ref
  31.0 0.0 copy-done.2
  31.0 0.0 copy-done.3
  31.0 99.9 %sum_attend.1 = (bf16[256,1024]{1,0:T(8,128)(2,1)S(1)}, bf16[256,512]{1,0:T(8,128)(2,1)S(1)}) custom-call(bf16[256,512]{1,0:T(8,128)(2,1)S(1)} %mix_scan.1.gated_ref, bf16[4,64,1024]{2,1,0:T(8,128)(2,1)S(1)} %all-to-all-done.share_ref, bf16[1024,2048]{1,0:T(8,128)(2,1)} %weight_ref.1, bf16[256,512]{1,0:T(8,128)(2,1)S(1)} %copy-done.2, ...), custom_call_target="tpu_custom_call" | custom-call | flops 1073741824 | bytes 4194304 | tf_op jit(solution)/shard_map/sum_attend/pallas_call | solution.py:356
  130.9 0.8 copy.17
  131.7 0.7 copy.18
  (2 shorter events, 0.0 us)
Async XLA Ops:
  0.6 28.2 %copy-start.5 = (f32[512,16]{0,1:T(8,128)S(1)}, f32[512,16]{0,1:T(8,128)}, u32[]{:S(2)}) copy-start(f32[512,16]{0,1:T(8,128)} %param.12) | copy-start | bytes 98308
  0.6 28.2 %copy-start.6 = (f32[512]{0:T(512)S(1)}, f32[512]{0:T(512)}, u32[]{:S(2)}) copy-start(f32[512]{0:T(512)} %param.13) | copy-start | bytes 6148
  0.7 30.3 %copy-start.2 = (bf16[256,512]{1,0:T(8,128)(2,1)S(1)}, bf16[256,512]{1,0:T(8,128)(2,1)}, u32[]{:S(2)}) copy-start(bf16[256,512]{1,0:T(8,128)(2,1)} %q_ref.1) | copy-start | bytes 786436
  0.7 30.3 %copy-start.3 = (bf16[256,512]{1,0:T(8,128)(2,1)S(1)}, bf16[256,512]{1,0:T(8,128)(2,1)}, u32[]{:S(2)}) copy-start(bf16[256,512]{1,0:T(8,128)(2,1)} %own_ref.1) | copy-start | bytes 786436
  2.6 28.3 %all-to-all-start = ((bf16[4,64,1024]{2,1,0:T(8,128)(2,1)}), bf16[4,64,1024]{2,1,0:T(8,128)(2,1)S(1)}, u32[]{:S(2)}, u32[]{:S(2)}) async-start(bf16[4,64,1024]{2,1,0:T(8,128)(2,1)} %bitcast.11), calls=%async_computation | async-start | bytes 1048576 | tf_op jit(solution)/shard_map/all_to_all | solution.py:409
  8.2 3.9 %collective-permute-start = (bf16[3,16,512]{2,1,0:T(8,128)(2,1)S(1)}, bf16[3,16,512]{2,1,0:T(8,128)(2,1)S(1)}, u32[]{:S(2)}, u32[]{:S(2)}) collective-permute-start(bf16[3,16,512]{2,1,0:T(8,128)(2,1)S(1)} %slice.3), channel_id=1, source_target_pairs={{0,4},{4,8},{8,12},{12,16},{16,20},{20,24},{24,28},{1,5},{5,9},{9,... | collective-permute-start | bytes 147464 | tf_op jit(solution)/shard_map/ppermute | solution.py:20
  12.1 1.1 copy-start
  13.2 0.8 copy-start.1
  14.0 0.8 copy-start.4

commit v4 on v3

--- a/solution.py
+++ b/solution.py
@@ -183,13 +183,26 @@
             device_id_type=pl.DeviceIdType.MESH,
         )
 
-    def full_copy(away):
+    chips = ctx // 2
+    chip, core = lax.div(me, 2), lax.rem(me, 2)
+    sibling = 2 * chip + 1 - core
+
+    def full_copy(index):
+        if index == 0:
+            source, block, target = share_ref, me, sibling
+        elif index < chips:
+            source, block = share_ref, me
+            target = 2 * lax.rem(chip + index, chips) + core
+        else:
+            away = index - chips + 1
+            block = 2 * lax.rem(chip + chips - away, chips) + core
+            source, target = full.at[:, block], sibling
         return pltpu.make_async_remote_copy(
-            src_ref=share_ref,
-            dst_ref=full.at[:, me],
-            send_sem=full_sems.at[0, away],
-            recv_sem=full_sems.at[1, away],
-            device_id={"ctx": lax.rem(me + away, ctx)},
+            src_ref=source,
+            dst_ref=full.at[:, block],
+            send_sem=full_sems.at[0, index],
+            recv_sem=full_sems.at[1, index],
+            device_id={"ctx": target},
             device_id_type=pl.DeviceIdType.MESH,
         )
 
@@ -205,21 +218,26 @@
 
     for away in range(1, tp):
         gat_copy(away).start()
-    for away in range(1, ctx):
-        full_copy(away).start()
+    for index in range(1, chips):
+        full_copy(index).start()
+    full_copy(0).start()
 
     def key_on(ahead, unused):
         key_copy(ahead).start()
         return unused
 
-    lax.fori_loop(1, ctx - me, key_on, 0)
     gat[lane] = gated_ref[...]
     full[:, me] = share_ref[...]
     keys[0] = own_ref[...]
+    for index in range(1, chips):
+        full_copy(index).wait_recv()
+        full_copy(index + chips - 1).start()
+    lax.fori_loop(1, ctx - me, key_on, 0)
     for away in range(1, tp):
         gat_copy(away).wait_recv()
-    for away in range(1, ctx):
-        full_copy(away).wait_recv()
+    full_copy(0).wait_recv()
+    for index in range(chips, 2 * chips - 1):
+        full_copy(index).wait_recv()
     chans, wide = gat.shape[2], full.shape[3]
     tile = min(wide, 256)
     for at in range(0, wide, tile):
@@ -339,8 +357,8 @@
         lax.fori_loop(1, ctx - me, sent, 0)
     for away in range(1, tp):
         gat_copy(away).wait_send()
-    for away in range(1, ctx):
-        full_copy(away).wait_send()
+    for index in range(2 * chips - 1):
+        full_copy(index).wait_send()
 
     def key_sent(ahead, unused):
         key_copy(ahead).wait_send()

time: 134 us -> 113 us (0.84)
  Pallas kernels: 104 us -> 83.6 us
    pallas_call x1, Pallas kernels: 99.9 us -> 79.4 us  [sum_and_attend(): pl.pallas_call(functools.partial(attend_kernel, ctx, tp), in_specs=[pl.Bl...]
  transfers between devices with their start and end apart: 2 -> 2, of which waited for: 1 -> 1; matrix products, arithmetic and copies ran while one was open for 1% -> 2% of each run, Pallas kernels for 3% -> 4%
where the time goes in v4:
time: 113 us; the launch traced here: 112 us
  Pallas kernels  83.6 us (74%)
  blocking collectives  11.9 us (11%)
  local copies, waits for them, and re-layouts  6.97 us (6%)
  starting transfers between devices  6.04 us (5%)
  waiting for transfers between devices  1.77 us (2%)
    pallas_call x1, Pallas kernels, sum_and_attend(): pl.pallas_call(functools.partial(attend_kernel, ctx, tp), in_specs=[pl.Bl...  79.4 us
    all_gather x1, blocking collectives, hyena_gated(): ends = lax.all_gather(end_state, 'ctx')  11.9 us
    all_to_all x1, starting transfers between devices, shards(): share = lax.all_to_all(share, 'tp', split_axis=0, concat_axis=0, tiled=True)  4.76 us
    unnamed x16, local copies, waits for them, and re-layouts  4.2 us
  transfers between devices with their start and end apart: 2, of which 1 were waited for; matrix products, arithmetic and copies ran while one was open for 2% of the time, Pallas kernels for 4%

profile of v4, /device:TPU:15, one launch (start us, length us, event | category | flops | bytes accessed | tf_op | source)
XLA Modules:
  0.0 111.9 jit_solution(16451920168313296972)
XLA Ops:
  0.6 0.0 copy-start.5
  0.6 0.0 copy-start.6
  0.7 0.0 copy-start.2
  0.7 0.0 copy-start.3
  0.7 1.1 %constant_dynamic-slice_fusion = bf16[64,4096]{1,0:T(8,128)(2,1)S(1)} fusion(bf16[512,4096]{1,0:T(8,128)(2,1)} %param.14, s32[]{:T(128)S(6)} %select_n.8), kind=kLoop, calls=%fused_computation.5 | loop fusion | bytes 1048580 | tf_op jit(solution)/shard_map/dynamic_slice | solution.py:425
  1.8 0.8 copy.14
  2.6 4.8 %all-to-all-start = ((bf16[4,64,1024]{2,1,0:T(8,128)(2,1)}), bf16[4,64,1024]{2,1,0:T(8,128)(2,1)S(1)}, u32[]{:S(2)}, u32[]{:S(2)}) async-start(bf16[4,64,1024]{2,1,0:T(8,128)(2,1)} %bitcast.11), calls=%async_computation | async-start | bytes 1048576 | tf_op jit(solution)/shard_map/all_to_all | solution.py:427
  7.4 0.8 slice.3
  8.2 1.3 %collective-permute-start = (bf16[3,16,512]{2,1,0:T(8,128)(2,1)S(1)}, bf16[3,16,512]{2,1,0:T(8,128)(2,1)S(1)}, u32[]{:S(2)}, u32[]{:S(2)}) collective-permute-start(bf16[3,16,512]{2,1,0:T(8,128)(2,1)S(1)} %slice.3), channel_id=1, source_target_pairs={{0,4},{4,8},{8,12},{12,16},{16,20},{20,24},{24,28},{1,5},{5,9},{9,... | collective-permute-start | bytes 147464 | tf_op jit(solution)/shard_map/ppermute | solution.py:20
  9.5 0.8 bitcast_negate_fusion
  10.3 1.8 %collective-permute-done.prev_ref = bf16[3,16,512]{2,1,0:T(8,128)(2,1)S(1)} collective-permute-done((bf16[3,16,512]{2,1,0:T(8,128)(2,1)S(1)}, bf16[3,16,512]{2,1,0:T(8,128)(2,1)S(1)}, u32[]{:S(2)}, u32[]{:S(2)}) %collective-permute-start) | collective-permute-done | bytes 49184 | tf_op jit(solution)/shard_map/ppermute | solution.py:20
  12.1 0.0 copy-start
  12.1 1.1 %copy-done = bf16[3,256,512]{2,1,0:T(8,128)(2,1)S(1)} copy-done((bf16[3,256,512]{2,1,0:T(8,128)(2,1)S(1)}, bf16[3,256,512]{2,1,0:T(8,128)(2,1)}, u32[]{:S(2)}) %copy-start) | copy-done | bytes 786456
  13.2 0.0 copy-start.1
  13.2 0.8 copy-done.1
  14.0 0.0 copy-start.4
  14.0 0.8 copy-done.4
  14.8 2.1 %filter_scan.1 = (f32[256,512]{1,0:T(8,128)S(1)}, f32[256,512]{1,0:T(8,128)S(1)}, f32[128,512]{1,0:T(8,128)S(1)}, f32[16,512]{1,0:T(8,128)S(1)}) custom-call(bf16[3,16,512]{2,1,0:T(8,128)(2,1)S(1)} %collective-permute-done.prev_ref, bf16[3,256,512]{2,1,0:T(8,128)(2,1)S(1)} %copy-done, f32[3,7,512]{2,1,0:T(8,128)S(1)} %copy-done.4, f32[16,512]{1,0:T(8,128)S(1)} %bitcast.12), custom_call_target="tpu_custom_call" | custom-call | flops 20000000 | bytes 2500000 | tf_op jit(solution)/shard_map/filter_scan/pallas_call | solution.py:90
  16.9 11.9 %all-gather = f32[128,512]{1,0:T(8,128)S(1)} all-gather(f32[16,512]{1,0:T(8,128)S(1)} %get-tuple-element.9), channel_id=2, replica_groups=mesh['ctx'=8,'tp'=4] {'ctx'}, dimensions={0}, use_global_device_ids=true | all-gather | bytes 294912 | tf_op jit(solution)/shard_map/all_gather | solution.py:112
  28.7 0.1 select_reduce_fusion.inc_ref
  28.8 0.0 copy-done.5
  28.8 0.0 copy-done.6
  28.9 2.1 %mix_scan.1.gated_ref = bf16[256,512]{1,0:T(8,128)(2,1)S(1)} custom-call(f32[256,512]{1,0:T(8,128)S(1)} %get-tuple-element.6.gate_ref, f32[256,512]{1,0:T(8,128)S(1)} %get-tuple-element.7.u_ref, f32[128,512]{1,0:T(8,128)S(1)} %get-tuple-element.8.seg_ref, f32[16,512]{1,0:T(8,128)S(1)} %select_reduce_fusion.inc_ref, f32[16,512]{1,0:T(8,128)S(1)} %bitcast.13, ...), custom_call_target="tpu_custom_call" | custom-call | flops 20000000 | bytes 2500000 | tf_op jit(solution)/shard_map/mix_scan/pallas_call | solution.py:116
  30.9 0.0 all-to-all-done.share_ref
  31.0 0.0 copy-done.2
  31.0 0.0 copy-done.3
  31.0 79.4 %sum_attend.1 = (bf16[256,1024]{1,0:T(8,128)(2,1)S(1)}, bf16[256,512]{1,0:T(8,128)(2,1)S(1)}) custom-call(bf16[256,512]{1,0:T(8,128)(2,1)S(1)} %mix_scan.1.gated_ref, bf16[4,64,1024]{2,1,0:T(8,128)(2,1)S(1)} %all-to-all-done.share_ref, bf16[1024,2048]{1,0:T(8,128)(2,1)} %weight_ref.1, bf16[256,512]{1,0:T(8,128)(2,1)S(1)} %copy-done.2, ...), custom_call_target="tpu_custom_call" | custom-call | flops 1073741824 | bytes 4194304 | tf_op jit(solution)/shard_map/sum_attend/pallas_call | solution.py:374
  110.4 0.8 copy.17
  111.2 0.7 copy.18
  (2 shorter events, 0.0 us)
Async XLA Ops:
  0.6 28.2 %copy-start.5 = (f32[512,16]{0,1:T(8,128)S(1)}, f32[512,16]{0,1:T(8,128)}, u32[]{:S(2)}) copy-start(f32[512,16]{0,1:T(8,128)} %param.12) | copy-start | bytes 98308
  0.6 28.2 %copy-start.6 = (f32[512]{0:T(512)S(1)}, f32[512]{0:T(512)}, u32[]{:S(2)}) copy-start(f32[512]{0:T(512)} %param.13) | copy-start | bytes 6148
  0.7 30.3 %copy-start.2 = (bf16[256,512]{1,0:T(8,128)(2,1)S(1)}, bf16[256,512]{1,0:T(8,128)(2,1)}, u32[]{:S(2)}) copy-start(bf16[256,512]{1,0:T(8,128)(2,1)} %q_ref.1) | copy-start | bytes 786436
  0.7 30.3 %copy-start.3 = (bf16[256,512]{1,0:T(8,128)(2,1)S(1)}, bf16[256,512]{1,0:T(8,128)(2,1)}, u32[]{:S(2)}) copy-start(bf16[256,512]{1,0:T(8,128)(2,1)} %own_ref.1) | copy-start | bytes 786436
  2.6 28.3 %all-to-all-start = ((bf16[4,64,1024]{2,1,0:T(8,128)(2,1)}), bf16[4,64,1024]{2,1,0:T(8,128)(2,1)S(1)}, u32[]{:S(2)}, u32[]{:S(2)}) async-start(bf16[4,64,1024]{2,1,0:T(8,128)(2,1)} %bitcast.11), calls=%async_computation | async-start | bytes 1048576 | tf_op jit(solution)/shard_map/all_to_all | solution.py:427
  8.2 3.9 %collective-permute-start = (bf16[3,16,512]{2,1,0:T(8,128)(2,1)S(1)}, bf16[3,16,512]{2,1,0:T(8,128)(2,1)S(1)}, u32[]{:S(2)}, u32[]{:S(2)}) collective-permute-start(bf16[3,16,512]{2,1,0:T(8,128)(2,1)S(1)} %slice.3), channel_id=1, source_target_pairs={{0,4},{4,8},{8,12},{12,16},{16,20},{20,24},{24,28},{1,5},{5,9},{9,... | collective-permute-start | bytes 147464 | tf_op jit(solution)/shard_map/ppermute | solution.py:20
  12.1 1.1 %copy-start = (bf16[3,256,512]{2,1,0:T(8,128)(2,1)S(1)}, bf16[3,256,512]{2,1,0:T(8,128)(2,1)}, u32[]{:S(2)}) copy-start(bf16[3,256,512]{2,1,0:T(8,128)(2,1)} %streams_ref.1) | copy-start | bytes 2359300
  13.2 0.8 copy-start.1
  14.0 0.8 copy-start.4

commit v5 on v4

--- a/solution.py
+++ b/solution.py
@@ -206,25 +206,64 @@
             device_id_type=pl.DeviceIdType.MESH,
         )
 
-    def key_copy(ahead):
+    def later(buffer, sems, source, slot, index, target):
         return pltpu.make_async_remote_copy(
-            src_ref=own_ref,
-            dst_ref=keys.at[ahead],
-            send_sem=key_sems.at[0, ahead],
-            recv_sem=key_sems.at[1, ahead],
-            device_id={"ctx": lax.rem(me + ahead, ctx)},
-            device_id_type=pl.DeviceIdType.MESH,
-        )
+            src_ref=buffer(source),
+            dst_ref=buffer(slot),
+            send_sem=sems(0, index),
+            recv_sem=sems(1, slot),
+            device_id={"ctx": target},
+            device_id_type=pl.DeviceIdType.MESH,
+        )
+
+    def ahead(at, d):
+        return later(*at, 0, 2 * d, 2 * d, lax.rem(me + 2 * d, ctx))
+
+    def beside(at):
+        return later(*at, 0, 1, 0, sibling)
+
+    def onward(at, d):
+        return later(*at, 2 * d, 2 * d + 1 - 2 * core, 2 * d - 1, sibling)
+
+    def loop(first, last, act):
+        def body(i, unused):
+            act(i)
+            return unused
+
+        lax.fori_loop(first, last, body, 0)
+
+    def give(at):
+        loop(1, chips - chip, lambda d: ahead(at, d).start())
+        loop(0, 1 - core, lambda d: beside(at).start())
+
+    def relay(at):
+        def step(d):
+            ahead(at, d).wait_recv()
+            onward(at, d).start()
+
+        loop(1, chip + 1, step)
+
+    def odd(at, i):
+        return later(*at, 0, 2 * i + 1, 0, sibling)
+
+    def take(at):
+        loop(0, chip + core, lambda i: odd(at, i).wait_recv())
+
+    def given(at):
+        loop(1, chips - chip, lambda d: ahead(at, d).wait_send())
+        loop(0, 1 - core, lambda d: beside(at).wait_send())
+        loop(1, chip + 1, lambda d: onward(at, d).wait_send())
+
+    key_at = (lambda slot: keys.at[slot], lambda way, i: key_sems.at[way, i])
+
+    def val_at(head):
+        return (lambda slot: vals.at[slot, head], lambda way, i: val_sems.at[way, i, head])
 
     for away in range(1, tp):
         gat_copy(away).start()
     for index in range(1, chips):
         full_copy(index).start()
     full_copy(0).start()
-
-    def key_on(ahead, unused):
-        key_copy(ahead).start()
-        return unused
 
     gat[lane] = gated_ref[...]
     full[:, me] = share_ref[...]
@@ -232,7 +271,7 @@
     for index in range(1, chips):
         full_copy(index).wait_recv()
         full_copy(index + chips - 1).start()
-    lax.fori_loop(1, ctx - me, key_on, 0)
+    give(key_at)
     for away in range(1, tp):
         gat_copy(away).wait_recv()
     full_copy(0).wait_recv()
@@ -266,16 +305,6 @@
             send_sem=sum_sems.at[0, away - 1, head],
             recv_sem=sum_sems.at[1, away - 1, head],
             device_id={"tp": owner},
-            device_id_type=pl.DeviceIdType.MESH,
-        )
-
-    def val_copy(ahead, head):
-        return pltpu.make_async_remote_copy(
-            src_ref=vals.at[0, head],
-            dst_ref=vals.at[ahead, head],
-            send_sem=val_sems.at[0, ahead, head],
-            recv_sem=val_sems.at[1, ahead, head],
-            device_id={"ctx": lax.rem(me + ahead, ctx)},
             device_id_type=pl.DeviceIdType.MESH,
         )
 
@@ -321,9 +350,6 @@
         fold(0, True)
 
         def earlier(behind, unused):
-            if head == 0:
-                key_copy(behind).wait_recv()
-            val_copy(behind, head).wait_recv()
             fold(behind, False)
             return unused
 
@@ -337,34 +363,29 @@
             value = value + parts[away - 1, head].astype(jnp.float32)
         vals[0, head] = value.astype(jnp.bfloat16)
 
-        def hand_on(ahead, unused, head=head):
-            val_copy(ahead, head).start()
-            return unused
-
-        lax.fori_loop(1, ctx - me, hand_on, 0)
-        if head >= 1:
+        give(val_at(head))
+        if head == 0:
+            relay(key_at)
+            take(key_at)
+        else:
+            relay(val_at(head - 1))
+            take(val_at(head - 1))
             attend(head - 1)
+    relay(val_at(heads - 1))
+    take(val_at(heads - 1))
     attend(heads - 1)
 
     for head in range(heads):
         for away in range(1, tp):
             sum_copy(away, head).wait_send()
 
-        def sent(ahead, unused, head=head):
-            val_copy(ahead, head).wait_send()
-            return unused
-
-        lax.fori_loop(1, ctx - me, sent, 0)
+        given(val_at(head))
     for away in range(1, tp):
         gat_copy(away).wait_send()
     for index in range(2 * chips - 1):
         full_copy(index).wait_send()
 
-    def key_sent(ahead, unused):
-        key_copy(ahead).wait_send()
-        return unused
-
-    lax.fori_loop(1, ctx - me, key_sent, 0)
+    given(key_at)
 
 
 def sum_and_attend(gated, share, value_weight, queries, keys):

time: 113 us -> 107 us (0.947)
  Pallas kernels: 83.6 us -> 77.7 us
    pallas_call x1, Pallas kernels: 79.4 us -> 73.5 us  [sum_and_attend(): pl.pallas_call(functools.partial(attend_kernel, ctx, tp), in_specs=[pl.Bl...]
where the time goes in v5:
time: 107 us; the launch traced here: 106 us
  Pallas kernels  77.7 us (73%)
  blocking collectives  11.9 us (11%)
  local copies, waits for them, and re-layouts  6.97 us (7%)
  starting transfers between devices  6.04 us (6%)
  waiting for transfers between devices  1.77 us (2%)
    pallas_call x1, Pallas kernels, sum_and_attend(): pl.pallas_call(functools.partial(attend_kernel, ctx, tp), in_specs=[pl.Bl...  73.5 us
    all_gather x1, blocking collectives, hyena_gated(): ends = lax.all_gather(end_state, 'ctx')  11.9 us
    all_to_all x1, starting transfers between devices, shards(): share = lax.all_to_all(share, 'tp', split_axis=0, concat_axis=0, tiled=True)  4.76 us
    unnamed x16, local copies, waits for them, and re-layouts  4.2 us
  transfers between devices with their start and end apart: 2, of which 1 were waited for; matrix products, arithmetic and copies ran while one was open for 2% of the time, Pallas kernels for 4%

profile of v5, /device:TPU:15, one launch (start us, length us, event | category | flops | bytes accessed | tf_op | source)
XLA Modules:
  0.0 106.0 jit_solution(17304491147270760642)
XLA Ops:
  0.6 0.0 copy-start.5
  0.6 0.0 copy-start.6
  0.7 0.0 copy-start.2
  0.7 0.0 copy-start.3
  0.7 1.1 %constant_dynamic-slice_fusion = bf16[64,4096]{1,0:T(8,128)(2,1)S(1)} fusion(bf16[512,4096]{1,0:T(8,128)(2,1)} %param.14, s32[]{:T(128)S(6)} %select_n.8), kind=kLoop, calls=%fused_computation.5 | loop fusion | bytes 1048580 | tf_op jit(solution)/shard_map/dynamic_slice | solution.py:446
  1.8 0.8 copy.14
  2.6 4.8 %all-to-all-start = ((bf16[4,64,1024]{2,1,0:T(8,128)(2,1)}), bf16[4,64,1024]{2,1,0:T(8,128)(2,1)S(1)}, u32[]{:S(2)}, u32[]{:S(2)}) async-start(bf16[4,64,1024]{2,1,0:T(8,128)(2,1)} %bitcast.11), calls=%async_computation | async-start | bytes 1048576 | tf_op jit(solution)/shard_map/all_to_all | solution.py:448
  7.4 0.8 slice.3
  8.2 1.3 %collective-permute-start = (bf16[3,16,512]{2,1,0:T(8,128)(2,1)S(1)}, bf16[3,16,512]{2,1,0:T(8,128)(2,1)S(1)}, u32[]{:S(2)}, u32[]{:S(2)}) collective-permute-start(bf16[3,16,512]{2,1,0:T(8,128)(2,1)S(1)} %slice.3), channel_id=1, source_target_pairs={{0,4},{4,8},{8,12},{12,16},{16,20},{20,24},{24,28},{1,5},{5,9},{9,... | collective-permute-start | bytes 147464 | tf_op jit(solution)/shard_map/ppermute | solution.py:20
  9.5 0.8 bitcast_negate_fusion
  10.3 1.8 %collective-permute-done.prev_ref = bf16[3,16,512]{2,1,0:T(8,128)(2,1)S(1)} collective-permute-done((bf16[3,16,512]{2,1,0:T(8,128)(2,1)S(1)}, bf16[3,16,512]{2,1,0:T(8,128)(2,1)S(1)}, u32[]{:S(2)}, u32[]{:S(2)}) %collective-permute-start) | collective-permute-done | bytes 49184 | tf_op jit(solution)/shard_map/ppermute | solution.py:20
  12.1 0.0 copy-start
  12.1 1.1 %copy-done = bf16[3,256,512]{2,1,0:T(8,128)(2,1)S(1)} copy-done((bf16[3,256,512]{2,1,0:T(8,128)(2,1)S(1)}, bf16[3,256,512]{2,1,0:T(8,128)(2,1)}, u32[]{:S(2)}) %copy-start) | copy-done | bytes 786456
  13.2 0.0 copy-start.1
  13.2 0.8 copy-done.1
  14.0 0.0 copy-start.4
  14.0 0.8 copy-done.4
  14.8 2.1 %filter_scan.1 = (f32[256,512]{1,0:T(8,128)S(1)}, f32[256,512]{1,0:T(8,128)S(1)}, f32[128,512]{1,0:T(8,128)S(1)}, f32[16,512]{1,0:T(8,128)S(1)}) custom-call(bf16[3,16,512]{2,1,0:T(8,128)(2,1)S(1)} %collective-permute-done.prev_ref, bf16[3,256,512]{2,1,0:T(8,128)(2,1)S(1)} %copy-done, f32[3,7,512]{2,1,0:T(8,128)S(1)} %copy-done.4, f32[16,512]{1,0:T(8,128)S(1)} %bitcast.12), custom_call_target="tpu_custom_call" | custom-call | flops 20000000 | bytes 2500000 | tf_op jit(solution)/shard_map/filter_scan/pallas_call | solution.py:90
  16.9 11.9 %all-gather = f32[128,512]{1,0:T(8,128)S(1)} all-gather(f32[16,512]{1,0:T(8,128)S(1)} %get-tuple-element.9), channel_id=2, replica_groups=mesh['ctx'=8,'tp'=4] {'ctx'}, dimensions={0}, use_global_device_ids=true | all-gather | bytes 294912 | tf_op jit(solution)/shard_map/all_gather | solution.py:112
  28.7 0.1 select_reduce_fusion.inc_ref
  28.8 0.0 copy-done.5
  28.8 0.0 copy-done.6
  28.9 2.1 %mix_scan.1.gated_ref = bf16[256,512]{1,0:T(8,128)(2,1)S(1)} custom-call(f32[256,512]{1,0:T(8,128)S(1)} %get-tuple-element.6.gate_ref, f32[256,512]{1,0:T(8,128)S(1)} %get-tuple-element.7.u_ref, f32[128,512]{1,0:T(8,128)S(1)} %get-tuple-element.8.seg_ref, f32[16,512]{1,0:T(8,128)S(1)} %select_reduce_fusion.inc_ref, f32[16,512]{1,0:T(8,128)S(1)} %bitcast.13, ...), custom_call_target="tpu_custom_call" | custom-call | flops 20000000 | bytes 2500000 | tf_op jit(solution)/shard_map/mix_scan/pallas_call | solution.py:116
  30.9 0.0 all-to-all-done.share_ref
  31.0 0.0 copy-done.2
  31.0 0.0 copy-done.3
  31.0 73.5 %sum_attend.1 = (bf16[256,1024]{1,0:T(8,128)(2,1)S(1)}, bf16[256,512]{1,0:T(8,128)(2,1)S(1)}) custom-call(bf16[256,512]{1,0:T(8,128)(2,1)S(1)} %mix_scan.1.gated_ref, bf16[4,64,1024]{2,1,0:T(8,128)(2,1)S(1)} %all-to-all-done.share_ref, bf16[1024,2048]{1,0:T(8,128)(2,1)} %weight_ref.1, bf16[256,512]{1,0:T(8,128)(2,1)S(1)} %copy-done.2, ...), custom_call_target="tpu_custom_call" | custom-call | flops 1073741824 | bytes 4194304 | tf_op jit(solution)/shard_map/sum_attend/pallas_call | solution.py:395
  104.5 0.8 copy.17
  105.3 0.7 copy.18
  (2 shorter events, 0.0 us)
Async XLA Ops:
  0.6 28.2 %copy-start.5 = (f32[512,16]{0,1:T(8,128)S(1)}, f32[512,16]{0,1:T(8,128)}, u32[]{:S(2)}) copy-start(f32[512,16]{0,1:T(8,128)} %param.12) | copy-start | bytes 98308
  0.6 28.2 %copy-start.6 = (f32[512]{0:T(512)S(1)}, f32[512]{0:T(512)}, u32[]{:S(2)}) copy-start(f32[512]{0:T(512)} %param.13) | copy-start | bytes 6148
  0.7 30.3 %copy-start.2 = (bf16[256,512]{1,0:T(8,128)(2,1)S(1)}, bf16[256,512]{1,0:T(8,128)(2,1)}, u32[]{:S(2)}) copy-start(bf16[256,512]{1,0:T(8,128)(2,1)} %q_ref.1) | copy-start | bytes 786436
  0.7 30.3 %copy-start.3 = (bf16[256,512]{1,0:T(8,128)(2,1)S(1)}, bf16[256,512]{1,0:T(8,128)(2,1)}, u32[]{:S(2)}) copy-start(bf16[256,512]{1,0:T(8,128)(2,1)} %own_ref.1) | copy-start | bytes 786436
  2.6 28.3 %all-to-all-start = ((bf16[4,64,1024]{2,1,0:T(8,128)(2,1)}), bf16[4,64,1024]{2,1,0:T(8,128)(2,1)S(1)}, u32[]{:S(2)}, u32[]{:S(2)}) async-start(bf16[4,64,1024]{2,1,0:T(8,128)(2,1)} %bitcast.11), calls=%async_computation | async-start | bytes 1048576 | tf_op jit(solution)/shard_map/all_to_all | solution.py:448
  8.2 3.9 %collective-permute-start = (bf16[3,16,512]{2,1,0:T(8,128)(2,1)S(1)}, bf16[3,16,512]{2,1,0:T(8,128)(2,1)S(1)}, u32[]{:S(2)}, u32[]{:S(2)}) collective-permute-start(bf16[3,16,512]{2,1,0:T(8,128)(2,1)S(1)} %slice.3), channel_id=1, source_target_pairs={{0,4},{4,8},{8,12},{12,16},{16,20},{20,24},{24,28},{1,5},{5,9},{9,... | collective-permute-start | bytes 147464 | tf_op jit(solution)/shard_map/ppermute | solution.py:20
  12.1 1.1 %copy-start = (bf16[3,256,512]{2,1,0:T(8,128)(2,1)S(1)}, bf16[3,256,512]{2,1,0:T(8,128)(2,1)}, u32[]{:S(2)}) copy-start(bf16[3,256,512]{2,1,0:T(8,128)(2,1)} %streams_ref.1) | copy-start | bytes 2359300
  13.2 0.8 copy-start.1
  14.0 0.8 copy-start.4

commit v6 on v5

--- a/solution.py
+++ b/solution.py
@@ -364,16 +364,18 @@
         vals[0, head] = value.astype(jnp.bfloat16)
 
         give(val_at(head))
-        if head == 0:
-            relay(key_at)
-            take(key_at)
-        else:
-            relay(val_at(head - 1))
-            take(val_at(head - 1))
-            attend(head - 1)
+        relay(key_at if head == 0 else val_at(head - 1))
+        if head >= 2:
+            if head == 2:
+                take(key_at)
+            take(val_at(head - 2))
+            attend(head - 2)
     relay(val_at(heads - 1))
-    take(val_at(heads - 1))
-    attend(heads - 1)
+    if heads <= 2:
+        take(key_at)
+    for head in range(max(heads - 2, 0), heads):
+        take(val_at(head))
+        attend(head)
 
     for head in range(heads):
         for away in range(1, tp):

time: 107 us -> 108 us (level)
  no operation moved by 1% of the time
where the time goes in v6:
time: 108 us; the launch traced here: 107 us
  Pallas kernels  78.7 us (73%)
  blocking collectives  11.9 us (11%)
  local copies, waits for them, and re-layouts  6.97 us (6%)
  starting transfers between devices  6.04 us (6%)
  waiting for transfers between devices  1.77 us (2%)
    pallas_call x1, Pallas kernels, sum_and_attend(): pl.pallas_call(functools.partial(attend_kernel, ctx, tp), in_specs=[pl.Bl...  74.5 us
    all_gather x1, blocking collectives, hyena_gated(): ends = lax.all_gather(end_state, 'ctx')  11.9 us
    all_to_all x1, starting transfers between devices, shards(): share = lax.all_to_all(share, 'tp', split_axis=0, concat_axis=0, tiled=True)  4.76 us
    unnamed x16, local copies, waits for them, and re-layouts  4.2 us
  transfers between devices with their start and end apart: 2, of which 1 were waited for; matrix products, arithmetic and copies ran while one was open for 2% of the time, Pallas kernels for 4%

profile of v6, /device:TPU:15, one launch (start us, length us, event | category | flops | bytes accessed | tf_op | source)
XLA Modules:
  0.0 107.0 jit_solution(6746551780414318417)
XLA Ops:
  0.6 0.0 copy-start.5
  0.6 0.0 copy-start.6
  0.7 0.0 copy-start.2
  0.7 0.0 copy-start.3
  0.7 1.1 %constant_dynamic-slice_fusion = bf16[64,4096]{1,0:T(8,128)(2,1)S(1)} fusion(bf16[512,4096]{1,0:T(8,128)(2,1)} %param.14, s32[]{:T(128)S(6)} %select_n.8), kind=kLoop, calls=%fused_computation.5 | loop fusion | bytes 1048580 | tf_op jit(solution)/shard_map/dynamic_slice | solution.py:448
  1.8 0.8 copy.14
  2.6 4.8 %all-to-all-start = ((bf16[4,64,1024]{2,1,0:T(8,128)(2,1)}), bf16[4,64,1024]{2,1,0:T(8,128)(2,1)S(1)}, u32[]{:S(2)}, u32[]{:S(2)}) async-start(bf16[4,64,1024]{2,1,0:T(8,128)(2,1)} %bitcast.11), calls=%async_computation | async-start | bytes 1048576 | tf_op jit(solution)/shard_map/all_to_all | solution.py:450
  7.4 0.8 slice.3
  8.2 1.3 %collective-permute-start = (bf16[3,16,512]{2,1,0:T(8,128)(2,1)S(1)}, bf16[3,16,512]{2,1,0:T(8,128)(2,1)S(1)}, u32[]{:S(2)}, u32[]{:S(2)}) collective-permute-start(bf16[3,16,512]{2,1,0:T(8,128)(2,1)S(1)} %slice.3), channel_id=1, source_target_pairs={{0,4},{4,8},{8,12},{12,16},{16,20},{20,24},{24,28},{1,5},{5,9},{9,... | collective-permute-start | bytes 147464 | tf_op jit(solution)/shard_map/ppermute | solution.py:20
  9.5 0.8 bitcast_negate_fusion
  10.3 1.8 %collective-permute-done.prev_ref = bf16[3,16,512]{2,1,0:T(8,128)(2,1)S(1)} collective-permute-done((bf16[3,16,512]{2,1,0:T(8,128)(2,1)S(1)}, bf16[3,16,512]{2,1,0:T(8,128)(2,1)S(1)}, u32[]{:S(2)}, u32[]{:S(2)}) %collective-permute-start) | collective-permute-done | bytes 49184 | tf_op jit(solution)/shard_map/ppermute | solution.py:20
  12.1 0.0 copy-start
  12.1 1.1 %copy-done = bf16[3,256,512]{2,1,0:T(8,128)(2,1)S(1)} copy-done((bf16[3,256,512]{2,1,0:T(8,128)(2,1)S(1)}, bf16[3,256,512]{2,1,0:T(8,128)(2,1)}, u32[]{:S(2)}) %copy-start) | copy-done | bytes 786456
  13.2 0.0 copy-start.1
  13.2 0.8 copy-done.1
  14.0 0.0 copy-start.4
  14.0 0.8 copy-done.4
  14.8 2.1 %filter_scan.1 = (f32[256,512]{1,0:T(8,128)S(1)}, f32[256,512]{1,0:T(8,128)S(1)}, f32[128,512]{1,0:T(8,128)S(1)}, f32[16,512]{1,0:T(8,128)S(1)}) custom-call(bf16[3,16,512]{2,1,0:T(8,128)(2,1)S(1)} %collective-permute-done.prev_ref, bf16[3,256,512]{2,1,0:T(8,128)(2,1)S(1)} %copy-done, f32[3,7,512]{2,1,0:T(8,128)S(1)} %copy-done.4, f32[16,512]{1,0:T(8,128)S(1)} %bitcast.12), custom_call_target="tpu_custom_call" | custom-call | flops 20000000 | bytes 2500000 | tf_op jit(solution)/shard_map/filter_scan/pallas_call | solution.py:90
  16.9 11.9 %all-gather = f32[128,512]{1,0:T(8,128)S(1)} all-gather(f32[16,512]{1,0:T(8,128)S(1)} %get-tuple-element.9), channel_id=2, replica_groups=mesh['ctx'=8,'tp'=4] {'ctx'}, dimensions={0}, use_global_device_ids=true | all-gather | bytes 294912 | tf_op jit(solution)/shard_map/all_gather | solution.py:112
  28.7 0.1 select_reduce_fusion.inc_ref
  28.8 0.0 copy-done.5
  28.8 0.0 copy-done.6
  28.9 2.1 %mix_scan.1.gated_ref = bf16[256,512]{1,0:T(8,128)(2,1)S(1)} custom-call(f32[256,512]{1,0:T(8,128)S(1)} %get-tuple-element.6.gate_ref, f32[256,512]{1,0:T(8,128)S(1)} %get-tuple-element.7.u_ref, f32[128,512]{1,0:T(8,128)S(1)} %get-tuple-element.8.seg_ref, f32[16,512]{1,0:T(8,128)S(1)} %select_reduce_fusion.inc_ref, f32[16,512]{1,0:T(8,128)S(1)} %bitcast.13, ...), custom_call_target="tpu_custom_call" | custom-call | flops 20000000 | bytes 2500000 | tf_op jit(solution)/shard_map/mix_scan/pallas_call | solution.py:116
  30.9 0.0 all-to-all-done.share_ref
  31.0 0.0 copy-done.2
  31.0 0.0 copy-done.3
  31.0 74.5 %sum_attend.1 = (bf16[256,1024]{1,0:T(8,128)(2,1)S(1)}, bf16[256,512]{1,0:T(8,128)(2,1)S(1)}) custom-call(bf16[256,512]{1,0:T(8,128)(2,1)S(1)} %mix_scan.1.gated_ref, bf16[4,64,1024]{2,1,0:T(8,128)(2,1)S(1)} %all-to-all-done.share_ref, bf16[1024,2048]{1,0:T(8,128)(2,1)} %weight_ref.1, bf16[256,512]{1,0:T(8,128)(2,1)S(1)} %copy-done.2, ...), custom_call_target="tpu_custom_call" | custom-call | flops 1073741824 | bytes 4194304 | tf_op jit(solution)/shard_map/sum_attend/pallas_call | solution.py:397
  105.5 0.8 copy.17
  106.3 0.7 copy.18
  (2 shorter events, 0.0 us)
Async XLA Ops:
  0.6 28.2 %copy-start.5 = (f32[512,16]{0,1:T(8,128)S(1)}, f32[512,16]{0,1:T(8,128)}, u32[]{:S(2)}) copy-start(f32[512,16]{0,1:T(8,128)} %param.12) | copy-start | bytes 98308
  0.6 28.2 %copy-start.6 = (f32[512]{0:T(512)S(1)}, f32[512]{0:T(512)}, u32[]{:S(2)}) copy-start(f32[512]{0:T(512)} %param.13) | copy-start | bytes 6148
  0.7 30.3 %copy-start.2 = (bf16[256,512]{1,0:T(8,128)(2,1)S(1)}, bf16[256,512]{1,0:T(8,128)(2,1)}, u32[]{:S(2)}) copy-start(bf16[256,512]{1,0:T(8,128)(2,1)} %q_ref.1) | copy-start | bytes 786436
  0.7 30.3 %copy-start.3 = (bf16[256,512]{1,0:T(8,128)(2,1)S(1)}, bf16[256,512]{1,0:T(8,128)(2,1)}, u32[]{:S(2)}) copy-start(bf16[256,512]{1,0:T(8,128)(2,1)} %own_ref.1) | copy-start | bytes 786436
  2.6 28.3 %all-to-all-start = ((bf16[4,64,1024]{2,1,0:T(8,128)(2,1)}), bf16[4,64,1024]{2,1,0:T(8,128)(2,1)S(1)}, u32[]{:S(2)}, u32[]{:S(2)}) async-start(bf16[4,64,1024]{2,1,0:T(8,128)(2,1)} %bitcast.11), calls=%async_computation | async-start | bytes 1048576 | tf_op jit(solution)/shard_map/all_to_all | solution.py:450
  8.2 3.9 %collective-permute-start = (bf16[3,16,512]{2,1,0:T(8,128)(2,1)S(1)}, bf16[3,16,512]{2,1,0:T(8,128)(2,1)S(1)}, u32[]{:S(2)}, u32[]{:S(2)}) collective-permute-start(bf16[3,16,512]{2,1,0:T(8,128)(2,1)S(1)} %slice.3), channel_id=1, source_target_pairs={{0,4},{4,8},{8,12},{12,16},{16,20},{20,24},{24,28},{1,5},{5,9},{9,... | collective-permute-start | bytes 147464 | tf_op jit(solution)/shard_map/ppermute | solution.py:20
  12.1 1.1 %copy-start = (bf16[3,256,512]{2,1,0:T(8,128)(2,1)S(1)}, bf16[3,256,512]{2,1,0:T(8,128)(2,1)}, u32[]{:S(2)}) copy-start(bf16[3,256,512]{2,1,0:T(8,128)(2,1)} %streams_ref.1) | copy-start | bytes 2359300
  13.2 0.8 copy-start.1
  14.0 0.8 copy-start.4
